TPU v7x, 32 devices: a whole 2x2x4 slice. The times are simulated.
32 devices in a mesh: grp: 8 (over z, y), inner: 4 (over x, core).
Axes of the slice: x: 2, y: 2, z: 4, core: 2. Of those that a mesh axis runs over, the one named last changes fastest.
Arguments:
- b_tensor: bfloat16 [10, 256, 3072], P(None, ('grp', 'inner')), may hold values from -0.59765625 to 0.59765625
- occ_energy: float32 [10], replicated, may hold values from -2 to -0.5
- vir_energy: float32 [3072], replicated, may hold values from 0.5 to 4
- left_list: int32 [3], replicated, may hold values from 0 to 9
- right_occ: int32 [1], replicated, may hold values from 0 to 9
Outputs:
- gamma_aux: float32 [10, 256, 3072], P(None, ('grp', 'inner'))
Inputs may be any that keep to these rules, and one draw needn't show every extreme that they name: `left_list`: each entry is an occupied orbital of the window; a first orbital may equal the second, and first orbitals may repeat. `right_occ`: an occupied orbital of the window.
All inputs are finite; a program needn't handle non-finite values.
Results may differ from a plain program's by a relative error of at most 0.0023.
Values may be sent and summed in bfloat16 or wider, within the bound.
A program may use at most 128 MiB of HBM per device.

v0:
```python
import jax
import jax.numpy as jnp
from jax import lax
from jax.sharding import PartitionSpec as P


def body(b_tensor, occ_energy, vir_energy, left_list, right_occ):
    inner_size = lax.axis_size("inner")
    group_size = lax.axis_size("grp")
    occ_count = b_tensor.shape[0]
    virtuals = b_tensor.shape[2]
    row_count = virtuals // inner_size
    col_count = virtuals // group_size
    inner_rank = lax.axis_index("inner")
    group_rank = lax.axis_index("grp")
    vir_rows = lax.dynamic_slice_in_dim(vir_energy, inner_rank * row_count, row_count)
    vir_cols = lax.dynamic_slice_in_dim(vir_energy, group_rank * col_count, col_count)
    gamma_aux = jnp.zeros(b_tensor.shape, jnp.float32)
    orbitals = jnp.arange(occ_count, dtype=jnp.int32)
    second_occ = right_occ[0]
    block_right = lax.dynamic_index_in_dim(b_tensor, second_occ, 0, keepdims=False)
    right_full = lax.all_gather(block_right, "inner", axis=0, tiled=True)
    pair_total = left_list.shape[0]
    selectors = []
    shifts = []
    partials = []
    amp_list = []
    for pair_no in range(pair_total):
        left_occ = left_list[pair_no]
        block_left = lax.dynamic_index_in_dim(b_tensor, left_occ, 0, keepdims=False)
        left_rows = lax.all_to_all(block_left, "inner", split_axis=1, concat_axis=0, tiled=True)
        partial_value = lax.dot_general(
            left_rows, right_full, (((0,), (0,)), ((), ())), preferred_element_type=jnp.float32
        )
        shift_occ = occ_energy[left_occ] + occ_energy[second_occ]
        selectors.append((orbitals == left_occ).astype(jnp.float32))
        partials.append(partial_value)
        shifts.append(shift_occ)
    stacked = jnp.stack(partials, axis=0)
    shares_all = lax.psum_scatter(stacked, "grp", scatter_dimension=2, tiled=True)
    shift_all = jnp.stack(shifts, axis=0)
    denominator_all = shift_all[:, None, None] - vir_rows[None, :, None] - vir_cols[None, None, :]
    amp_tiles = (shares_all / denominator_all).astype(jnp.bfloat16)
    amp_whole = lax.all_gather(amp_tiles, "grp", axis=2, tiled=True)
    amp_list = [amp_whole[pair_no] for pair_no in range(pair_total)]
    for pair_no in range(pair_total):
        contrib = lax.dot_general(
            right_full,
            amp_list[pair_no],
            (((1,), (1,)), ((), ())),
            preferred_element_type=jnp.float32,
        )
        returned = lax.all_to_all(contrib, "inner", split_axis=0, concat_axis=1, tiled=True)
        gamma_aux = gamma_aux + selectors[pair_no][:, None, None] * returned[None]
    return gamma_aux


def solution(mesh):
    placed = (P(None, ("grp", "inner"), None), P(), P(), P(), P())
    return jax.shard_map(
        body, mesh=mesh, in_specs=placed, out_specs=P(None, ("grp", "inner"), None), check_vma=False
    )
```

profile of v0, /device:TPU:0, one launch (start us, length us, event | category | flops | bytes accessed | tf_op | source)
XLA Modules:
  0.0 745.9 jit_solution(13265645204235905528)
XLA Ops:
  6.5 1.4 fusion.13
  14.0 1.5 constant_dynamic-slice_fusion.2
  15.5 4.2 all-to-all-start.1
  19.7 5.9 all-gather
  25.6 0.0 all-to-all-done.1
  25.6 3.3 all-to-all-start
  28.9 5.1 convolution_bitcast_fusion.1
  34.0 0.0 all-to-all-done
  34.0 3.3 all-to-all-start.2
  37.3 0.0 reduce-scatter.2.cloned.1.call-start
  37.3 5.1 convolution_bitcast_fusion.2
  42.4 0.0 all-to-all-done.2
  42.4 0.0 copy-start
  42.4 1.4 convolution_bitcast_fusion
  43.8 2.3 copy-done
  46.1 13.4 %pad_maximum_fusion = f32[3,768,3072]{2,1,0:T(8,128)} fusion(f32[1,768,3072]{2,1,0:T(8,128)S(1)} %convolution_bitcast_fusion, f32[1,768,3072]{2,1,0:T(8,128)} %convolution_bitcast_fusion.1, f32[1,768,3072]{2,1,0:T(8,128)S(1)} %copy-done), kind=kLoop, calls=%fused_computation | loop fusion | flops 14155776 | bytes 56623104 | tf_op jit(solution)/shard_map/stack | solution.py:39
  59.5 0.0 copy-start.1
  59.5 0.0 copy-start.2
  59.5 0.0 reduce-scatter.2.cloned.1.call-update
  59.6 0.0 all-gather.3.cloned.1.call-start
  59.6 0.6 copy-done.1
  60.2 0.6 fusion.12
  64.3 0.0 copy-done.2
  64.3 0.1 dynamic_slice.41
  64.4 0.1 dynamic_slice.42
  64.5 0.1 pad_maximum_fusion.1
  64.5 0.1 broadcast_subtract_fusion
  64.6 446.9 %reduce-scatter.2.cloned.1.call-done = f32[3,768,384]{2,1,0:T(8,128)} async-done(((f32[3,768,3072]{2,1,0:T(8,128)}), f32[3,768,384]{2,1,0:T(8,128)}) %reduce-scatter.2.cloned.1.call-update) | async-done | bytes 3538960 | tf_op jit(solution)/shard_map/reduce_scatter | solution.py:40
  511.5 3.8 divide_convert_fusion
  515.2 0.0 all-gather.3.cloned.1.call-update
  515.3 1.2 compare_convert_fusion
  516.5 193.8 %all-gather.3.cloned.1.call-done = bf16[3,768,3072]{2,1,0:T(8,128)(2,1)} async-done(((bf16[3,768,384]{2,1,0:T(8,128)(2,1)}), bf16[3,768,3072]{2,1,0:T(8,128)(2,1)}) %all-gather.3.cloned.1.call-update) | async-done | bytes 14155792 | tf_op jit(solution)/shard_map/all_gather | solution.py:44
  710.3 4.5 fusion.2
  714.7 3.3 all-to-all-start.3
  718.0 4.5 fusion.1
  722.5 0.0 all-to-all-done.3
  722.5 3.3 all-to-all-start.4
  725.8 4.5 fusion
  730.3 0.0 all-to-all-done.4
  730.3 3.3 all-to-all-start.5
  733.6 0.6 compare_convert_fusion.2
  734.2 3.6 all-to-all-done.5
  737.9 1.2 multiply_add_fusion
Async XLA Ops:
  15.5 10.1 %all-to-all-start.1 = ((bf16[8,4,768]{2,0,1:T(8,128)(2,1)}), bf16[8,4,768]{2,0,1:T(8,128)(2,1)S(1)}, u32[]{:S(2)}, u32[]{:S(2)}) async-start(bf16[8,4,768]{2,0,1:T(8,128)(2,1)} %bitcast.9), calls=%async_computation.1 | async-start | bytes 98304 | tf_op jit(solution)/shard_map/all_to_all | solution.py:31
  25.6 8.4 %all-to-all-start = ((bf16[8,4,768]{2,0,1:T(8,128)(2,1)}), bf16[8,4,768]{2,0,1:T(8,128)(2,1)S(1)}, u32[]{:S(2)}, u32[]{:S(2)}) async-start(bf16[8,4,768]{2,0,1:T(8,128)(2,1)} %bitcast.3), calls=%async_computation | async-start | bytes 98304 | tf_op jit(solution)/shard_map/all_to_all | solution.py:31
  34.0 8.4 %all-to-all-start.2 = ((bf16[8,4,768]{2,0,1:T(8,128)(2,1)}), bf16[8,4,768]{2,0,1:T(8,128)(2,1)S(1)}, u32[]{:S(2)}, u32[]{:S(2)}) async-start(bf16[8,4,768]{2,0,1:T(8,128)(2,1)} %bitcast.14), calls=%async_computation.2 | async-start | bytes 98304 | tf_op jit(solution)/shard_map/all_to_all | solution.py:31
  37.3 474.2 %reduce-scatter.2.cloned.1.call-start = ((), (), s32[]{:S(2)}) async-start(), calls=%async_computation.7 | async-start | bytes 31850496 | tf_op jit(solution)/shard_map/reduce_scatter | solution.py:40
  42.4 3.7 copy-start
  59.5 0.7 copy-start.1
  59.5 4.8 copy-start.2
  59.6 650.7 %all-gather.3.cloned.1.call-start = ((), (), s32[]{:S(2)}) async-start(), calls=%async_computation.8 | async-start | bytes 15925248 | tf_op jit(solution)/shard_map/all_gather | solution.py:44
  714.7 7.8 %all-to-all-start.3 = ((f32[4,8,768]{2,1,0:T(8,128)}), f32[4,8,768]{2,1,0:T(8,128)S(1)}, u32[]{:S(2)}, u32[]{:S(2)}) async-start(f32[4,8,768]{2,1,0:T(8,128)} %fusion.2), calls=%async_computation.4 | async-start | bytes 196608 | tf_op jit(solution)/shard_map/all_to_all | solution.py:53
  722.5 7.8 %all-to-all-start.4 = ((f32[4,8,768]{2,1,0:T(8,128)}), f32[4,8,768]{2,1,0:T(8,128)S(1)}, u32[]{:S(2)}, u32[]{:S(2)}) async-start(f32[4,8,768]{2,1,0:T(8,128)} %fusion.1), calls=%async_computation.5 | async-start | bytes 196608 | tf_op jit(solution)/shard_map/all_to_all | solution.py:53
  730.3 7.6 %all-to-all-start.5 = ((f32[4,8,768]{2,1,0:T(8,128)}), f32[4,8,768]{2,1,0:T(8,128)S(1)}, u32[]{:S(2)}, u32[]{:S(2)}) async-start(f32[4,8,768]{2,1,0:T(8,128)} %fusion), calls=%async_computation.6 | async-start | bytes 196608 | tf_op jit(solution)/shard_map/all_to_all | solution.py:53
Sparse Core Ops, SparseCore 0:
  59.7 451.7 reduce-scatter.1
  515.4 194.8 all-gather.2
where the time goes:
time: 747 us; the launch traced here: 746 us
  waiting for transfers between devices  644 us (86%)
  matrix products  25 us (3%)
  between operations  23.1 us (3%)
  starting transfers between devices  20.8 us (3%)
  other arithmetic  20.3 us (3%)
    reduce_scatter x1, waiting for transfers between devices, body(): lax.psum_scatter(stacked, 'grp', scatter_dimension=2, tiled=True)  447 us
    all_gather x1, waiting for transfers between devices, body(): amp_whole = lax.all_gather(amp_tiles, 'grp', axis=2, tiled=True)  194 us
  transfers between devices with their start and end apart: 8, of which 3 were waited for; matrix products, arithmetic and copies ran while one was open for 3% of the time, Pallas kernels for 0%

commit v1 on v0

--- a/solution.py
+++ b/solution.py
@@ -55,8 +55,52 @@
     return gamma_aux
 
 
+def body_rows(b_tensor, occ_energy, vir_energy, left_list, right_occ):
+    axes = ("grp", "inner")
+    devices = lax.axis_size("grp") * lax.axis_size("inner")
+    me = lax.axis_index("grp") * lax.axis_size("inner") + lax.axis_index("inner")
+    occ_count, aux_rows, virtuals = b_tensor.shape
+    pair_total = left_list.shape[0]
+    width = virtuals // devices
+    second_occ = right_occ[0]
+    block_right = lax.dynamic_index_in_dim(b_tensor, second_occ, 0, keepdims=False)
+    block_left = jnp.take(b_tensor, left_list, axis=0)
+    right_full = lax.all_gather(block_right, axes, axis=0, tiled=True)
+    left_cols = lax.all_to_all(block_left, axes, split_axis=2, concat_axis=1, tiled=True)
+    integral = lax.dot_general(
+        left_cols, right_full, (((1,), (0,)), ((), ())), preferred_element_type=jnp.float32
+    )
+    vir_rows = lax.dynamic_slice_in_dim(vir_energy, me * width, width)
+    shift = occ_energy[left_list] + occ_energy[second_occ]
+    denominator = shift[:, None, None] - vir_rows[None, :, None] - vir_energy[None, None, :]
+    amplitude = (integral / denominator).astype(jnp.bfloat16)
+    contrib = lax.dot_general(
+        amplitude, right_full, (((2,), (1,)), ((), ())), preferred_element_type=jnp.float32
+    )
+    returned = lax.all_to_all(contrib, axes, split_axis=2, concat_axis=1, tiled=True)
+    returned = jnp.swapaxes(returned, 1, 2)
+    selector = (jnp.arange(occ_count)[:, None] == left_list[None, :]).astype(jnp.float32)
+    gamma_aux = jnp.zeros(b_tensor.shape, jnp.float32)
+    for pair_no in range(pair_total):
+        gamma_aux = gamma_aux + selector[:, pair_no][:, None, None] * returned[pair_no][None]
+    return gamma_aux
+
+
+GATHER_BYTES = 4 * 2**20
+
+
 def solution(mesh):
     placed = (P(None, ("grp", "inner"), None), P(), P(), P(), P())
-    return jax.shard_map(
-        body, mesh=mesh, in_specs=placed, out_specs=P(None, ("grp", "inner"), None), check_vma=False
-    )
+
+    def program(b_tensor, *rest):
+        aux, virtuals = b_tensor.shape[1:]
+        fits = 2 * aux * virtuals <= GATHER_BYTES and virtuals % mesh.size == 0
+        return jax.shard_map(
+            body_rows if fits else body,
+            mesh=mesh,
+            in_specs=placed,
+            out_specs=P(None, ("grp", "inner"), None),
+            check_vma=False,
+        )(b_tensor, *rest)
+
+    return program

time: 747 us -> 100 us (0.13)
  waiting for transfers between devices: 644 us -> 46.8 us
  matrix products: 25 us -> 3.11 us
  other arithmetic: 20.3 us -> 3.38 us
  local copies, waits for them, and re-layouts: 6.49 us -> 21.4 us
  starting transfers between devices: 20.8 us -> 10.8 us
  between operations: 23.1 us -> 14.2 us
    reduce_scatter x1 -> x0, waiting for transfers between devices: 447 us -> none  [body(): lax.psum_scatter(stacked, 'grp', scatter_dimension=2, tiled=True)]
    all_gather x1, waiting for transfers between devices: 194 us -> 24.9 us  [body_rows(): right_full = lax.all_gather(block_right, axes, axis=0, tiled=True)]
    dot_general x6 -> x1, matrix products: 25 us -> 3.11 us  [body_rows(): lax.dot_general(amplitude, right_full, (((2,), (1,)), ((), ())), preferre...]
    all_to_all x6 -> x2, waiting for transfers between devices: 3.64 us -> 21.9 us  [the longest x1 15.5 us: body_rows(): lax.all_to_all(contrib, axes, split_axis=2, concat_axis=1, tiled=True)]
    another operation x2 -> x0, other arithmetic: 13.5 us -> none  [the longest x1 13.4 us: body(): stacked = jnp.stack(partials, axis=0)]
    all_to_all x6 -> x2, starting transfers between devices: 20.7 us -> 10.8 us  [the longest x1 7.3 us: body_rows(): lax.all_to_all(block_left, axes, split_axis=2, concat_axis=1, tiled=True)]
  transfers between devices with their start and end apart: 8 -> 3, of which waited for: 3 -> 3; matrix products, arithmetic and copies ran while one was open for 3% -> 21% of each run, Pallas kernels for 0% -> 0%
where the time goes in v1:
time: 100 us; the launch traced here: 99.7 us
  waiting for transfers between devices  46.8 us (47%)
  local copies, waits for them, and re-layouts  21.4 us (21%)
  between operations  14.2 us (14%)
  starting transfers between devices  10.8 us (11%)
  other arithmetic  3.38 us (3%)
  matrix products  3.11 us (3%)
    all_gather x1, waiting for transfers between devices, body_rows(): right_full = lax.all_gather(block_right, axes, axis=0, tiled=True)  24.9 us
    all_to_all x1, waiting for transfers between devices, body_rows(): lax.all_to_all(contrib, axes, split_axis=2, concat_axis=1, tiled=True)  15.5 us
    unnamed x10, local copies, waits for them, and re-layouts  9.98 us
    all_to_all x1, starting transfers between devices, body_rows(): lax.all_to_all(block_left, axes, split_axis=2, concat_axis=1, tiled=True)  7.3 us
    all_to_all x1, waiting for transfers between devices, body_rows(): lax.all_to_all(block_left, axes, split_axis=2, concat_axis=1, tiled=True)  6.41 us
    all_to_all x1, local copies, waits for them, and re-layouts, body_rows(): lax.all_to_all(block_left, axes, split_axis=2, concat_axis=1, tiled=True)  4.08 us
    select_n x1, local copies, waits for them, and re-layouts, body_rows(): block_left = jnp.take(b_tensor, left_list, axis=0)  3.51 us
    all_to_all x1, starting transfers between devices, body_rows(): lax.all_to_all(contrib, axes, split_axis=2, concat_axis=1, tiled=True)  3.48 us
  transfers between devices with their start and end apart: 3, of which 3 were waited for; matrix products, arithmetic and copies ran while one was open for 21% of the time, Pallas kernels for 0%

profile of v1, /device:TPU:0, one launch (start us, length us, event | category | flops | bytes accessed | tf_op | source)
XLA Modules:
  0.0 99.7 jit_solution(1322126641412413584)
XLA Ops:
  6.5 0.0 copy-start
  6.5 0.0 all-gather.3.cloned.1.call-start
  7.3 0.3 copy-done
  7.6 0.6 constant_dynamic-slice_fusion
  8.2 0.0 all-gather.3.cloned.1.call-update
  8.2 0.7 compare_select_fusion
  8.9 0.6 gather_fusion
  9.5 0.7 compare_and_fusion
  10.1 0.1 broadcast_select_fusion
  10.2 3.5 %copy.14 = bf16[3,8,3072]{1,0,2:T(4,128)(2,1)} copy(bf16[3,8,3072]{2,1,0:T(8,128)(2,1)S(1)} %broadcast_select_fusion) | data formatting | bytes 294912 | tf_op jit(solution)/shard_map/jit(_take)/select_n | solution.py:67
  13.7 0.0 copy-start.1
  13.7 0.0 copy-start.3
  13.7 5.8 %reshape.64 = bf16[32,2,1152]{2,1,0:T(2,128)(2,1)} reshape(bf16[3072,3,8]{2,1,0:T(4,128)(2,1)} %bitcast.44) | data formatting | bytes 294912
  19.5 7.3 %all-to-all-start = ((bf16[32,2,1152]{2,1,0:T(2,128)(2,1)}), bf16[32,2,1152]{2,1,0:T(2,128)(2,1)S(1)}, u32[]{:S(2)}, u32[]{:S(2)}) async-start(bf16[32,2,1152]{2,1,0:T(2,128)(2,1)} %reshape.64), calls=%async_computation | async-start | bytes 294912 | tf_op jit(solution)/shard_map/all_to_all | solution.py:69
  26.8 0.0 copy-done.1
  26.8 0.6 dynamic_slice.11
  27.4 0.6 gather_fusion.1
  28.0 0.6 broadcast_add_fusion
  28.7 0.0 copy-done.3
  28.7 0.1 dynamic_slice.12
  28.8 0.1 broadcast_subtract_fusion
  28.9 6.4 %all-to-all-done = bf16[32,2,1152]{2,1,0:T(2,128)(2,1)S(1)} async-done(((bf16[32,2,1152]{2,1,0:T(2,128)(2,1)}), bf16[32,2,1152]{2,1,0:T(2,128)(2,1)S(1)}, u32[]{:S(2)}, u32[]{:S(2)}) %all-to-all-start) | async-done | bytes 147488 | tf_op jit(solution)/shard_map/all_to_all | solution.py:69
  35.3 3.9 %reshape.65 = bf16[3072,3,8]{2,1,0:T(4,128)(2,1)} reshape(bf16[32,2,1152]{2,1,0:T(2,128)(2,1)S(1)} %all-to-all-done) | data formatting | bytes 294912
  39.2 4.1 %copy.15 = bf16[3,8,32,96]{3,1,2,0:T(8,128)(2,1)S(1)} copy(bf16[3,8,32,96]{1,0,3,2:T(4,128)(2,1)} %bitcast.45) | data formatting | bytes 294912 | tf_op jit(solution)/shard_map/all_to_all | solution.py:69
  43.2 24.9 %all-gather.3.cloned.1.call-done = bf16[1,256,3072]{2,1,0:T(8,128)(2,1)} async-done(((bf16[1,8,3072]{2,1,0:T(8,128)(2,1)}), bf16[1,256,3072]{2,1,0:T(8,128)(2,1)}) %all-gather.3.cloned.1.call-update) | async-done | bytes 1572880 | tf_op jit(solution)/shard_map/all_gather | solution.py:68
  68.2 3.1 %fusion.1 = f32[3,96,256]{2,1,0:T(8,128)S(1)} fusion(bf16[1,256,3072]{2,1,0:T(8,128)(2,1)} %all-gather.3.cloned.1.call-done, f32[3072]{0:T(1024)S(1)} %copy-done.3, f32[3,96]{1,0:T(4,128)S(1)} %broadcast_subtract_fusion, bf16[3,8,32,96]{3,1,2,0:T(8,128)(2,1)S(1)} %copy.15), kind=kOutput, calls=%fused_computation.4 | convolution fusion | flops 908623872 | bytes 2028672 | tf_op jit(solution)/shard_map/dot_general | solution.py:77
  71.3 0.0 copy-start.2
  71.3 1.0 %copy.17 = f32[3,96,256]{1,0,2:T(4,128)} copy(f32[3,96,256]{2,1,0:T(8,128)S(1)} %fusion.1) | data formatting | bytes 589824 | tf_op jit(solution)/shard_map/dot_general | solution.py:77
  72.3 3.5 %all-to-all-start.1 = ((f32[3,96,256]{1,0,2:T(4,128)}), f32[3,96,256]{1,0,2:T(4,128)S(1)}, u32[]{:S(2)}, u32[]{:S(2)}) async-start(f32[3,96,256]{1,0,2:T(4,128)} %copy.17), calls=%async_computation.1 | async-start | bytes 1048576 | tf_op jit(solution)/shard_map/all_to_all | solution.py:80
  75.8 0.0 copy-done.2
  75.8 0.1 fusion.8
  75.9 15.5 %all-to-all-done.1 = f32[3,96,256]{1,0,2:T(4,128)S(1)} async-done(((f32[3,96,256]{1,0,2:T(4,128)}), f32[3,96,256]{1,0,2:T(4,128)S(1)}, u32[]{:S(2)}, u32[]{:S(2)}) %all-to-all-start.1) | async-done | bytes 294944 | tf_op jit(solution)/shard_map/all_to_all | solution.py:80
  91.4 0.1 copy.19
  91.4 0.2 all_to_all.33
  91.7 1.2 %multiply_add_fusion = f32[10,8,3072]{2,1,0:T(8,128)} fusion(f32[8,3072]{1,0:T(8,128)S(1)} %get-tuple-element.6, f32[10]{0:T(128)S(1)} %get-tuple-element.9, f32[8,3072]{1,0:T(8,128)S(1)} %get-tuple-element.7, f32[10]{0:T(128)S(1)} %get-tuple-element.10, f32[8,3072]{1,0:T(8,128)S(1)} %get-tuple-element.5, f32[10]{0:T(128)S(1)} %get-tuple-element.8), kind=kLoop, calls=%fused_computation.7 | loop fusion | flops 1228800 | bytes 1278072 | tf_op jit(solution)/shard_map/add | solution.py:85
  (4 shorter events, 0.1 us)
Async XLA Ops:
  6.5 1.0 %copy-start = (bf16[10,8,3072]{2,1,0:T(8,128)(2,1)S(1)}, bf16[10,8,3072]{2,1,0:T(8,128)(2,1)}, u32[]{:S(2)}) copy-start(bf16[10,8,3072]{2,1,0:T(8,128)(2,1)} %param.5) | copy-start | bytes 1474564
  6.5 61.6 %all-gather.3.cloned.1.call-start = ((), (), s32[]{:S(2)}) async-start(), calls=%async_computation.2 | async-start | bytes 1622016 | tf_op jit(solution)/shard_map/all_gather | solution.py:68
  13.7 13.1 %copy-start.1 = (f32[10]{0:T(128)S(1)}, f32[10]{0:T(128)}, u32[]{:S(2)}) copy-start(f32[10]{0:T(128)} %param.6) | copy-start | bytes 124
  13.7 15.0 %copy-start.3 = (f32[3072]{0:T(1024)S(1)}, f32[3072]{0:T(1024)}, u32[]{:S(2)}) copy-start(f32[3072]{0:T(1024)} %param.7) | copy-start | bytes 36868
  19.5 15.8 %all-to-all-start = ((bf16[32,2,1152]{2,1,0:T(2,128)(2,1)}), bf16[32,2,1152]{2,1,0:T(2,128)(2,1)S(1)}, u32[]{:S(2)}, u32[]{:S(2)}) async-start(bf16[32,2,1152]{2,1,0:T(2,128)(2,1)} %reshape.64), calls=%async_computation | async-start | bytes 294912 | tf_op jit(solution)/shard_map/all_to_all | solution.py:69
  71.3 4.5 %copy-start.2 = (s32[3]{0:T(128)S(1)}, s32[3]{0:T(128)}, u32[]{:S(2)}) copy-start(s32[3]{0:T(128)} %param.8) | copy-start | bytes 40
  72.3 19.0 %all-to-all-start.1 = ((f32[3,96,256]{1,0,2:T(4,128)}), f32[3,96,256]{1,0,2:T(4,128)S(1)}, u32[]{:S(2)}, u32[]{:S(2)}) async-start(f32[3,96,256]{1,0,2:T(4,128)} %copy.17), calls=%async_computation.1 | async-start | bytes 1048576 | tf_op jit(solution)/shard_map/all_to_all | solution.py:80
Sparse Core Ops, SparseCore 0:
  10.2 57.8 all-gather.2

commit v2 on v0

--- a/solution.py
+++ b/solution.py
@@ -1,7 +1,12 @@
 import jax
 import jax.numpy as jnp
 from jax import lax
+from jax.experimental import pallas as pl
+from jax.experimental.pallas import tpu as pltpu
 from jax.sharding import PartitionSpec as P
+
+MESH = pl.DeviceIdType.MESH
+LANES = 128
 
 
 def body(b_tensor, occ_energy, vir_energy, left_list, right_occ):
@@ -55,8 +60,307 @@
     return gamma_aux
 
 
+def place(grp, inner):
+    return grp // 2, grp % 2, inner // 2, inner % 2
+
+
+def tile_owner(tile):
+    grp = tile // 3
+    slot = tile % 3
+    idle = 2 * ((grp // 2 + grp % 2) % 2) + 1
+    return grp, slot + jnp.where(slot >= idle, 1, 0)
+
+
+def flip_z(z, step):
+    return (z, z + 1 - 2 * (z % 2), (z + 2) % 4, 3 - z)[step]
+
+
+def kernel(
+    b_ref, occ_ref, vir_ref, left_ref, right_ref, out_ref,
+    own, sib, pair_rows, full, left_cols, left_rows, contrib,
+    swap_send, swap_recv, gather_send, gather_recv, left_send, left_recv, out_send, out_recv,
+):
+    grp, inner = lax.axis_index("grp"), lax.axis_index("inner")
+    z, y, x, core = place(grp, inner)
+    me = grp * 4 + inner
+    chip = grp * 2 + x
+    pairs = out_ref.shape[0]
+    virtuals = full.shape[1]
+    half = virtuals // 2
+    quarter = virtuals // 4
+    tiles = virtuals // LANES
+
+    barrier = pltpu.get_barrier_semaphore()
+
+    @pl.loop(1, 32)
+    def _(step):
+        other = (me + step) % 32
+        pl.semaphore_signal(barrier, inc=1, device_id=(other // 4, other % 4), device_id_type=MESH)
+
+    second = right_ref[0]
+    own[pl.ds(0, 8), :] = b_ref[second]
+    for pair in range(pairs):
+        own[pl.ds(8 * pair + 8, 8), :] = b_ref[left_ref[pair]]
+    pl.semaphore_wait(barrier, 31)
+
+    sibling = (grp, inner + 1 - 2 * core)
+    swap = pltpu.make_async_remote_copy(
+        src_ref=own, dst_ref=sib, send_sem=swap_send, recv_sem=swap_recv, device_id=sibling, device_id_type=MESH
+    )
+    swap.start()
+    swap.wait_recv()
+
+    def merge(low, high):
+        for block in range(pairs + 1):
+            pair_rows[block, pl.ds(0, 8), :] = low[pl.ds(8 * block, 8), :]
+            pair_rows[block, pl.ds(8, 8), :] = high[pl.ds(8 * block, 8), :]
+
+    @pl.when(core == 0)
+    def _():
+        merge(own, sib)
+
+    @pl.when(core == 1)
+    def _():
+        merge(sib, own)
+
+    full[pl.ds(pl.multiple_of(chip * 16, 16), 16), :] = pair_rows[0]
+
+    my_col = core * half
+    x_side = (grp, (1 - x) * 2 + core)
+    y_side = (z * 2 + 1 - y, inner)
+    started = []
+
+    def send(slot, z_of, y_of, x_of, first, count, target):
+        row = pl.multiple_of(((z_of * 2 + y_of) * 2 + x_of) * 16, 16)
+        piece = full.at[pl.ds(row, 16), pl.ds(pl.multiple_of(first, LANES), count)]
+        copy = pltpu.make_async_remote_copy(
+            src_ref=piece, dst_ref=piece, send_sem=gather_send.at[slot], recv_sem=gather_recv.at[slot],
+            device_id=target, device_id_type=MESH,
+        )
+        copy.start()
+        started.append(copy)
+
+    def arrived(slot, z_of, y_of, x_of, first, count):
+        row = pl.multiple_of(((z_of * 2 + y_of) * 2 + x_of) * 16, 16)
+        piece = full.at[pl.ds(row, 16), pl.ds(pl.multiple_of(first, LANES), count)]
+        pltpu.make_async_remote_copy(
+            src_ref=piece, dst_ref=piece, send_sem=gather_send.at[slot], recv_sem=gather_recv.at[slot],
+            device_id=sibling, device_id_type=MESH,
+        ).wait_recv()
+
+    Z, X1, Y1, X2, Y2, CZ, CX, CY, CD = 0, 4, 8, 12, 16, 20, 24, 28, 32
+
+    def spread(step):
+        z_of = flip_z(z, step)
+        send(X1 + step, z_of, y, x, my_col, half, x_side)
+        send(Y1 + step, z_of, y, x, my_col, half, y_side)
+
+    for step in (1, 2, 3):
+        send(Z + step, z, y, x, my_col, half, (flip_z(z, step) * 2 + y, inner))
+    spread(0)
+
+    chip_rows = pl.ds(pl.multiple_of(chip * 16, 16), 16)
+
+    def left_copy(index):
+        tile = 2 * index + core
+        to_grp, to_inner = tile_owner(tile)
+        copy = pltpu.make_async_remote_copy(
+            src_ref=pair_rows.at[pl.ds(1, pairs), :, pl.ds(pl.multiple_of(tile * LANES, LANES), LANES)],
+            dst_ref=left_cols.at[:, chip_rows, :],
+            send_sem=left_send.at[index],
+            recv_sem=left_recv.at[chip],
+            device_id=(to_grp, to_inner),
+            device_id_type=MESH,
+        )
+        return to_grp * 2 + to_inner // 2 != chip, copy
+
+    @pl.loop(0, tiles // 2)
+    def _(step):
+        index = (step + 3 * (grp // 2)) % (tiles // 2)
+        away, copy = left_copy(index)
+
+        @pl.when(away)
+        def _():
+            copy.start()
+
+    def relay(step):
+        z_of = flip_z(z, step)
+        arrived(X1 + step, z_of, y, 1 - x, my_col, half)
+        send(Y2 + step, z_of, y, 1 - x, my_col, quarter, y_side)
+        send(CX + step, z_of, y, 1 - x, my_col, half, sibling)
+        arrived(Y1 + step, z_of, 1 - y, x, my_col, half)
+        send(X2 + step, z_of, 1 - y, x, my_col + quarter, quarter, x_side)
+        send(CY + step, z_of, 1 - y, x, my_col, half, sibling)
+
+    def finish(step):
+        z_of = flip_z(z, step)
+        arrived(Y2 + step, z_of, 1 - y, 1 - x, my_col, quarter)
+        arrived(X2 + step, z_of, 1 - y, 1 - x, my_col + quarter, quarter)
+        send(CD + step, z_of, 1 - y, 1 - x, my_col, half, sibling)
+
+    for step in (1, 2, 3):
+        z_of = flip_z(z, step)
+        arrived(Z + step, z_of, y, x, my_col, half)
+        spread(step)
+        send(CZ + step, z_of, y, x, my_col, half, sibling)
+        relay(step - 1)
+        if step > 1:
+            finish(step - 2)
+    relay(3)
+    finish(2)
+    finish(3)
+    other_col = (1 - core) * half
+    for step in range(4):
+        z_of = flip_z(z, step)
+        if step:
+            arrived(CZ + step, z_of, y, x, other_col, half)
+        arrived(CX + step, z_of, y, 1 - x, other_col, half)
+        arrived(CY + step, z_of, 1 - y, x, other_col, half)
+        arrived(CD + step, z_of, 1 - y, 1 - x, other_col, half)
+
+    idle = 2 * ((z + y) % 2) + 1
+    my_tile = grp * 3 + inner - jnp.where(inner > idle, 1, 0)
+    my_lanes = pl.ds(pl.multiple_of(my_tile * LANES, LANES), LANES)
+
+    def out_copy(step):
+        other = (me + step) % 32
+        return pltpu.make_async_remote_copy(
+            src_ref=contrib.at[:, pl.ds(pl.multiple_of(other * 8, 8), 8), :],
+            dst_ref=out_ref.at[:, :, my_lanes],
+            send_sem=out_send.at[step],
+            recv_sem=out_recv.at[my_tile],
+            device_id=(other // 4, other % 4),
+            device_id_type=MESH,
+        )
+
+    @pl.when(inner != idle)
+    def _():
+        left_cols[:, chip_rows, :] = pair_rows[pl.ds(1, pairs), :, my_lanes]
+
+        @pl.loop(1, 16)
+        def _(step):
+            source = (chip + step) % 16
+            pltpu.make_async_remote_copy(
+                src_ref=pair_rows.at[pl.ds(1, pairs), :, pl.ds(0, LANES)],
+                dst_ref=left_cols.at[:, pl.ds(pl.multiple_of(source * 16, 16), 16), :],
+                send_sem=left_send.at[0],
+                recv_sem=left_recv.at[source],
+                device_id=sibling,
+                device_id_type=MESH,
+            ).wait_recv()
+
+        vir_cols = jnp.transpose(jnp.broadcast_to(vir_ref[:, my_lanes], (LANES, LANES)))[:, :1]
+        shifts = []
+        for pair in range(pairs):
+            left_rows[pl.ds(pair * LANES, LANES), :] = jnp.transpose(left_cols[pair])
+            shifts.append((occ_ref[left_ref[pair]] + occ_ref[second]) - vir_cols)
+        shift = jnp.concatenate(shifts, axis=0)
+        contrib[...] = jnp.zeros_like(contrib)
+        wide = 4 * LANES
+
+        @pl.loop(0, virtuals // wide)
+        def _(part):
+            columns = pl.ds(pl.multiple_of(part * wide, wide), wide)
+            block = full[:, columns]
+            integral = jnp.dot(left_rows[...], block, preferred_element_type=jnp.float32)
+            amplitude = (integral / (shift - vir_ref[:, columns])).astype(jnp.bfloat16)
+            for pair in range(pairs):
+                contrib[pair] += lax.dot_general(
+                    block, amplitude[pair * LANES : (pair + 1) * LANES], (((1,), (1,)), ((), ())),
+                    preferred_element_type=jnp.float32,
+                )
+
+        out_ref[:, :, my_lanes] = contrib[:, pl.ds(pl.multiple_of(me * 8, 8), 8), :]
+
+        @pl.loop(1, 32)
+        def _(step):
+            out_copy(step).start()
+
+    swap.wait_send()
+    for copy in started:
+        copy.wait_send()
+
+    @pl.loop(0, tiles // 2)
+    def _(index):
+        away, copy = left_copy(index)
+
+        @pl.when(away)
+        def _():
+            copy.wait_send()
+
+    @pl.loop(0, tiles)
+    def _(tile):
+        from_grp, from_inner = tile_owner(tile)
+
+        @pl.when(from_grp * 4 + from_inner != me)
+        def _():
+            pltpu.make_async_remote_copy(
+                src_ref=contrib.at[:, pl.ds(0, 8), :],
+                dst_ref=out_ref.at[:, :, pl.ds(pl.multiple_of(tile * LANES, LANES), LANES)],
+                send_sem=out_send.at[0],
+                recv_sem=out_recv.at[tile],
+                device_id=sibling,
+                device_id_type=MESH,
+            ).wait_recv()
+
+    @pl.when(inner != idle)
+    def _():
+        @pl.loop(1, 32)
+        def _(step):
+            out_copy(step).wait_send()
+
+
+def body_tiles(b_tensor, occ_energy, vir_energy, left_list, right_occ):
+    occ_count, aux_rows, virtuals = b_tensor.shape
+    pairs = left_list.shape[0]
+    aux = 32 * aux_rows
+    vmem, smem = pl.BlockSpec(memory_space=pltpu.VMEM), pl.BlockSpec(memory_space=pltpu.SMEM)
+    dma = pltpu.SemaphoreType.DMA
+    returned = pl.pallas_call(
+        kernel,
+        out_shape=jax.ShapeDtypeStruct((pairs, aux_rows, virtuals), jnp.float32),
+        in_specs=[vmem, smem, vmem, smem, smem],
+        out_specs=vmem,
+        scratch_shapes=[
+            pltpu.VMEM(((pairs + 1) * aux_rows, virtuals), jnp.bfloat16),
+            pltpu.VMEM(((pairs + 1) * aux_rows, virtuals), jnp.bfloat16),
+            pltpu.VMEM((pairs + 1, 2 * aux_rows, virtuals), jnp.bfloat16),
+            pltpu.VMEM((aux, virtuals), jnp.bfloat16),
+            pltpu.VMEM((pairs, aux, LANES), jnp.bfloat16),
+            pltpu.VMEM((pairs * LANES, aux), jnp.bfloat16),
+            pltpu.VMEM((pairs, aux, LANES), jnp.float32),
+            dma, dma, dma((36,)), dma((36,)), dma((virtuals // LANES,)), dma((16,)),
+            dma((32,)), dma((virtuals // LANES,)),
+        ],
+        compiler_params=pltpu.CompilerParams(
+            collective_id=0, has_side_effects=True, vmem_limit_bytes=32 * 2**20
+        ),
+        cost_estimate=pl.CostEstimate(
+            flops=4 * pairs * aux * virtuals * LANES, bytes_accessed=2 * occ_count * aux_rows * virtuals, transcendentals=0
+        ),
+    )(b_tensor, occ_energy, vir_energy.reshape(1, virtuals), left_list, right_occ)
+    selector = (jnp.arange(occ_count)[:, None] == left_list[None, :]).astype(jnp.float32)
+    gamma_aux = jnp.zeros(b_tensor.shape, jnp.float32)
+    for pair_no in range(pairs):
+        gamma_aux = gamma_aux + selector[:, pair_no][:, None, None] * returned[pair_no][None]
+    return gamma_aux
+
+
 def solution(mesh):
     placed = (P(None, ("grp", "inner"), None), P(), P(), P(), P())
-    return jax.shard_map(
-        body, mesh=mesh, in_specs=placed, out_specs=P(None, ("grp", "inner"), None), check_vma=False
-    )
+    plan = body
+    if mesh.shape["grp"] == 8 and mesh.shape["inner"] == 4:
+        plan = body_tiles
+
+    def program(b_tensor, *rest):
+        aux, virtuals = b_tensor.shape[1:]
+        fits = aux == 256 and virtuals == 3072
+        return jax.shard_map(
+            plan if fits else body,
+            mesh=mesh,
+            in_specs=placed,
+            out_specs=P(None, ("grp", "inner"), None),
+            check_vma=False,
+        )(b_tensor, *rest)
+
+    return program

time: 747 us -> 41.2 us (0.06)
  the two profiles are of different devices: /device:TPU:0 before, /device:TPU:29 now
where the time goes in v2:
time: 41.2 us; the launch traced here: 41 us
  Pallas kernels  36.7 us (89%)
  local copies, waits for them, and re-layouts  2.35 us (6%)
  other arithmetic  1.25 us (3%)
  between operations  0.69 us (2%)
    pallas_call x1, Pallas kernels, body_tiles(): pl.pallas_call(kernel, out_shape=jax.ShapeDtypeStruct((pairs, aux_rows, v...  36.7 us
    unnamed x8, local copies, waits for them, and re-layouts  2.32 us
    add x1, other arithmetic, body_tiles(): gamma_aux + selector[:, pair_no][:, None, None] * returned[pair_no][None]  1.18 us

profile of v2, /device:TPU:29, one launch (start us, length us, event | category | flops | bytes accessed | tf_op | source)
XLA Modules:
  0.0 41.0 jit_solution(14180243607179307825)
XLA Ops:
  0.7 0.0 copy-start
  0.7 0.0 copy-start.2
  0.7 0.6 %copy-done = s32[3]{0:T(128)S(1)} copy-done((s32[3]{0:T(128)S(1)}, s32[3]{0:T(128)}, u32[]{:S(2)}) %copy-start) | copy-done | bytes 36
  1.3 0.1 fusion
  1.4 0.0 copy-start.3
  1.4 0.0 copy-done.2
  1.4 0.7 %copy-done.3 = f32[10]{0:T(128)S(1)} copy-done((f32[10]{0:T(128)S(1)}, f32[10]{0:T(128)}, u32[]{:S(2)}) %copy-start.3) | copy-done | bytes 64
  2.0 0.0 copy-start.1
  2.0 1.0 %copy-done.1 = bf16[10,8,3072]{2,1,0:T(8,128)(2,1)S(1)} copy-done((bf16[10,8,3072]{2,1,0:T(8,128)(2,1)S(1)}, bf16[10,8,3072]{2,1,0:T(8,128)(2,1)}, u32[]{:S(2)}) %copy-start.1) | copy-done | bytes 491544
  3.1 36.7 %shard_map.55 = f32[3,8,3072]{2,1,0:T(8,128)S(1)} custom-call(bf16[10,8,3072]{2,1,0:T(8,128)(2,1)S(1)} %copy-done.1, f32[10]{0:T(128)S(1)} %copy-done.3, f32[1,3072]{1,0:T(1,128)S(1)} %bitcast.13, s32[3]{0:T(128)S(1)} %copy-done, s32[1]{0:T(128)S(6)} %copy.6.right_ref), custom_call_target="tpu_custom_call" | custom-call | flops 1207959552 | bytes 491520 | tf_op jit(solution)/shard_map/pallas_call | solution.py:319
  39.8 1.2 %multiply_add_fusion = f32[10,8,3072]{2,1,0:T(8,128)} fusion(f32[8,3072]{1,0:T(8,128)S(1)} %get-tuple-element.6, f32[10]{0:T(128)S(1)} %get-tuple-element.9, f32[8,3072]{1,0:T(8,128)S(1)} %get-tuple-element.7, f32[10]{0:T(128)S(1)} %get-tuple-element.10, f32[8,3072]{1,0:T(8,128)S(1)} %get-tuple-element.5, f32[10]{0:T(128)S(1)} %get-tuple-element.8), kind=kLoop, calls=%fused_computation | loop fusion | flops 1228800 | bytes 1278072 | tf_op jit(solution)/shard_map/add | solution.py:345
  (2 shorter events, 0.0 us)
Async XLA Ops:
  0.7 0.7 %copy-start = (s32[3]{0:T(128)S(1)}, s32[3]{0:T(128)}, u32[]{:S(2)}) copy-start(s32[3]{0:T(128)} %left_ref.1) | copy-start | bytes 40
  0.7 0.7 %copy-start.2 = (f32[3072]{0:T(1024)S(1)}, f32[3072]{0:T(1024)}, u32[]{:S(2)}) copy-start(f32[3072]{0:T(1024)} %param.7) | copy-start | bytes 36868
  1.4 0.7 %copy-start.3 = (f32[10]{0:T(128)S(1)}, f32[10]{0:T(128)}, u32[]{:S(2)}) copy-start(f32[10]{0:T(128)} %occ_ref.1) | copy-start | bytes 124
  2.0 1.0 %copy-start.1 = (bf16[10,8,3072]{2,1,0:T(8,128)(2,1)S(1)}, bf16[10,8,3072]{2,1,0:T(8,128)(2,1)}, u32[]{:S(2)}) copy-start(bf16[10,8,3072]{2,1,0:T(8,128)(2,1)} %b_ref.1) | copy-start | bytes 1474564

commit v3 on v2

--- a/solution.py
+++ b/solution.py
@@ -76,8 +76,8 @@
 
 
 def kernel(
-    b_ref, occ_ref, vir_ref, left_ref, right_ref, out_ref,
-    own, sib, pair_rows, full, left_cols, left_rows, contrib,
+    b_hbm, occ_hbm, vir_hbm, left_hbm, right_hbm, gamma_ref,
+    b_ref, occ_ref, vir_ref, left_ref, right_ref, input_sem, out_ref, own, sib, pair_rows, full, left_cols, left_rows, contrib,
     swap_send, swap_recv, gather_send, gather_recv, left_send, left_recv, out_send, out_recv,
 ):
     grp, inner = lax.axis_index("grp"), lax.axis_index("inner")
@@ -90,6 +90,10 @@
     quarter = virtuals // 4
     tiles = virtuals // LANES
 
+    inputs = ((b_hbm, b_ref), (occ_hbm, occ_ref), (vir_hbm, vir_ref), (left_hbm, left_ref), (right_hbm, right_ref))
+    fetches = [pltpu.make_async_copy(a, b, input_sem.at[n]) for n, (a, b) in enumerate(inputs)]
+    for fetch in fetches:
+        fetch.start()
     barrier = pltpu.get_barrier_semaphore()
 
     @pl.loop(1, 32)
@@ -97,6 +101,8 @@
         other = (me + step) % 32
         pl.semaphore_signal(barrier, inc=1, device_id=(other // 4, other % 4), device_id_type=MESH)
 
+    for fetch in fetches:
+        fetch.wait()
     second = right_ref[0]
     own[pl.ds(0, 8), :] = b_ref[second]
     for pair in range(pairs):
@@ -255,20 +261,21 @@
             left_rows[pl.ds(pair * LANES, LANES), :] = jnp.transpose(left_cols[pair])
             shifts.append((occ_ref[left_ref[pair]] + occ_ref[second]) - vir_cols)
         shift = jnp.concatenate(shifts, axis=0)
-        contrib[...] = jnp.zeros_like(contrib)
         wide = 4 * LANES
-
-        @pl.loop(0, virtuals // wide)
-        def _(part):
-            columns = pl.ds(pl.multiple_of(part * wide, wide), wide)
+        total = jnp.zeros((pairs * LANES, full.shape[0]), jnp.float32)
+        for part in range(virtuals // wide):
+            columns = pl.ds(part * wide, wide)
             block = full[:, columns]
             integral = jnp.dot(left_rows[...], block, preferred_element_type=jnp.float32)
-            amplitude = (integral / (shift - vir_ref[:, columns])).astype(jnp.bfloat16)
-            for pair in range(pairs):
-                contrib[pair] += lax.dot_general(
-                    block, amplitude[pair * LANES : (pair + 1) * LANES], (((1,), (1,)), ((), ())),
-                    preferred_element_type=jnp.float32,
-                )
+            denominator = shift - vir_ref[:, columns]
+            inverse = pl.reciprocal(denominator, approx=True)
+            inverse = inverse * (2.0 - denominator * inverse)
+            amplitude = (integral * inverse).astype(jnp.bfloat16)
+            total += lax.dot_general(
+                amplitude, block, (((1,), (1,)), ((), ())), preferred_element_type=jnp.float32
+            )
+        for pair in range(pairs):
+            contrib[pair] = jnp.transpose(total[pair * LANES : (pair + 1) * LANES])
 
         out_ref[:, :, my_lanes] = contrib[:, pl.ds(pl.multiple_of(me * 8, 8), 8), :]
 
@@ -303,6 +310,12 @@
                 device_id_type=MESH,
             ).wait_recv()
 
+    for orbital in range(gamma_ref.shape[0]):
+        row = jnp.where(left_ref[0] == orbital, out_ref[0], 0.0)
+        for pair in range(1, pairs):
+            row += jnp.where(left_ref[pair] == orbital, out_ref[pair], 0.0)
+        gamma_ref[orbital] = row
+
     @pl.when(inner != idle)
     def _():
         @pl.loop(1, 32)
@@ -314,14 +327,21 @@
     occ_count, aux_rows, virtuals = b_tensor.shape
     pairs = left_list.shape[0]
     aux = 32 * aux_rows
-    vmem, smem = pl.BlockSpec(memory_space=pltpu.VMEM), pl.BlockSpec(memory_space=pltpu.SMEM)
+    hbm, vmem = pl.BlockSpec(memory_space=pltpu.HBM), pl.BlockSpec(memory_space=pltpu.VMEM)
     dma = pltpu.SemaphoreType.DMA
-    returned = pl.pallas_call(
+    return pl.pallas_call(
         kernel,
-        out_shape=jax.ShapeDtypeStruct((pairs, aux_rows, virtuals), jnp.float32),
-        in_specs=[vmem, smem, vmem, smem, smem],
+        out_shape=jax.ShapeDtypeStruct(b_tensor.shape, jnp.float32),
+        in_specs=[hbm] * 5,
         out_specs=vmem,
         scratch_shapes=[
+            pltpu.VMEM(b_tensor.shape, jnp.bfloat16),
+            pltpu.SMEM(occ_energy.shape, jnp.float32),
+            pltpu.VMEM((1, virtuals), jnp.float32),
+            pltpu.SMEM(left_list.shape, jnp.int32),
+            pltpu.SMEM(right_occ.shape, jnp.int32),
+            dma((5,)),
+            pltpu.VMEM((pairs, aux_rows, virtuals), jnp.float32),
             pltpu.VMEM(((pairs + 1) * aux_rows, virtuals), jnp.bfloat16),
             pltpu.VMEM(((pairs + 1) * aux_rows, virtuals), jnp.bfloat16),
             pltpu.VMEM((pairs + 1, 2 * aux_rows, virtuals), jnp.bfloat16),
@@ -333,17 +353,12 @@
             dma((32,)), dma((virtuals // LANES,)),
         ],
         compiler_params=pltpu.CompilerParams(
-            collective_id=0, has_side_effects=True, vmem_limit_bytes=32 * 2**20
+            collective_id=0, has_side_effects=True, vmem_limit_bytes=60 * 2**20
         ),
         cost_estimate=pl.CostEstimate(
             flops=4 * pairs * aux * virtuals * LANES, bytes_accessed=2 * occ_count * aux_rows * virtuals, transcendentals=0
         ),
     )(b_tensor, occ_energy, vir_energy.reshape(1, virtuals), left_list, right_occ)
-    selector = (jnp.arange(occ_count)[:, None] == left_list[None, :]).astype(jnp.float32)
-    gamma_aux = jnp.zeros(b_tensor.shape, jnp.float32)
-    for pair_no in range(pairs):
-        gamma_aux = gamma_aux + selector[:, pair_no][:, None, None] * returned[pair_no][None]
-    return gamma_aux
 
 
 def solution(mesh):

time: 41.2 us -> 38.7 us (0.939)
  other arithmetic: 1.25 us -> 0 us
  Pallas kernels: 36.7 us -> 35.7 us
    add x1 -> x0, other arithmetic: 1.18 us -> none  [body_tiles(): gamma_aux + selector[:, pair_no][:, None, None] * returned[pair_no][None]]
    pallas_call x1, Pallas kernels: 36.7 us -> 35.7 us  [body_tiles(): pl.pallas_call(kernel, out_shape=jax.ShapeDtypeStruct(b_tensor.shape, jnp...]
    unnamed x8 -> x1, local copies, waits for them, and re-layouts: 2.32 us -> 2.22 us
where the time goes in v3:
time: 38.7 us; the launch traced here: 38.6 us
  Pallas kernels  35.7 us (92%)
  local copies, waits for them, and re-layouts  2.22 us (6%)
  between operations  0.66 us (2%)
    pallas_call x1, Pallas kernels, body_tiles(): pl.pallas_call(kernel, out_shape=jax.ShapeDtypeStruct(b_tensor.shape, jnp...  35.7 us
    unnamed x1, local copies, waits for them, and re-layouts  2.22 us

profile of v3, /device:TPU:29, one launch (start us, length us, event | category | flops | bytes accessed | tf_op | source)
XLA Modules:
  0.0 38.6 jit_solution(5087402296302513842)
XLA Ops:
  0.7 35.7 %shard_map.55 = f32[10,8,3072]{2,1,0:T(8,128)} custom-call(bf16[10,8,3072]{2,1,0:T(8,128)(2,1)} %b_hbm.1, f32[10]{0:T(128)} %occ_hbm.1, f32[1,3072]{1,0:T(1,128)} %bitcast.1, s32[3]{0:T(128)} %left_hbm.1, s32[1]{0:T(128)S(6)} %copy.7.right_hbm), custom_call_target="tpu_custom_call" | custom-call | flops 1207959552 | bytes 491520 | tf_op jit(solution)/shard_map/pallas_call | solution.py:332
  36.3 2.2 %copy.8 = f32[10,8,3072]{2,1,0:T(8,128)} copy(f32[10,8,3072]{2,1,0:T(8,128)} %shard_map.55) | data formatting | bytes 1966080

commit v4 on v3

--- a/solution.py
+++ b/solution.py
@@ -76,8 +76,8 @@
 
 
 def kernel(
-    b_hbm, occ_hbm, vir_hbm, left_hbm, right_hbm, gamma_ref,
-    b_ref, occ_ref, vir_ref, left_ref, right_ref, input_sem, out_ref, own, sib, pair_rows, full, left_cols, left_rows, contrib,
+    b_hbm, occ_hbm, vir_hbm, left_hbm, right_hbm, out_ref,
+    b_ref, occ_ref, vir_ref, left_ref, right_ref, input_sem, own, sib, folded, pair_rows, full, left_cols, left_rows, contrib,
     swap_send, swap_recv, gather_send, gather_recv, left_send, left_recv, out_send, out_recv,
 ):
     grp, inner = lax.axis_index("grp"), lax.axis_index("inner")
@@ -85,9 +85,9 @@
     me = grp * 4 + inner
     chip = grp * 2 + x
     pairs = out_ref.shape[0]
-    virtuals = full.shape[1]
-    half = virtuals // 2
-    quarter = virtuals // 4
+    half = full.shape[2]
+    virtuals = 2 * half
+    quarter = half // 2
     tiles = virtuals // LANES
 
     inputs = ((b_hbm, b_ref), (occ_hbm, occ_ref), (vir_hbm, vir_ref), (left_hbm, left_ref), (right_hbm, right_ref))
@@ -104,6 +104,9 @@
     for fetch in fetches:
         fetch.wait()
     second = right_ref[0]
+    folded[pl.ds(0, 8), :] = b_ref[second, :, pl.ds(0, half)]
+    folded[pl.ds(8, 8), :] = b_ref[second, :, pl.ds(half, half)]
+    full[me] = folded[...]
     own[pl.ds(0, 8), :] = b_ref[second]
     for pair in range(pairs):
         own[pl.ds(8 * pair + 8, 8), :] = b_ref[left_ref[pair]]
@@ -113,32 +116,13 @@
     swap = pltpu.make_async_remote_copy(
         src_ref=own, dst_ref=sib, send_sem=swap_send, recv_sem=swap_recv, device_id=sibling, device_id_type=MESH
     )
-    swap.start()
-    swap.wait_recv()
-
-    def merge(low, high):
-        for block in range(pairs + 1):
-            pair_rows[block, pl.ds(0, 8), :] = low[pl.ds(8 * block, 8), :]
-            pair_rows[block, pl.ds(8, 8), :] = high[pl.ds(8 * block, 8), :]
-
-    @pl.when(core == 0)
-    def _():
-        merge(own, sib)
-
-    @pl.when(core == 1)
-    def _():
-        merge(sib, own)
-
-    full[pl.ds(pl.multiple_of(chip * 16, 16), 16), :] = pair_rows[0]
-
-    my_col = core * half
+
     x_side = (grp, (1 - x) * 2 + core)
     y_side = (z * 2 + 1 - y, inner)
     started = []
 
     def send(slot, z_of, y_of, x_of, first, count, target):
-        row = pl.multiple_of(((z_of * 2 + y_of) * 2 + x_of) * 16, 16)
-        piece = full.at[pl.ds(row, 16), pl.ds(pl.multiple_of(first, LANES), count)]
+        piece = full.at[(z_of * 2 + y_of) * 4 + x_of * 2 + core, :, pl.ds(first, count)]
         copy = pltpu.make_async_remote_copy(
             src_ref=piece, dst_ref=piece, send_sem=gather_send.at[slot], recv_sem=gather_recv.at[slot],
             device_id=target, device_id_type=MESH,
@@ -146,9 +130,8 @@
         copy.start()
         started.append(copy)
 
-    def arrived(slot, z_of, y_of, x_of, first, count):
-        row = pl.multiple_of(((z_of * 2 + y_of) * 2 + x_of) * 16, 16)
-        piece = full.at[pl.ds(row, 16), pl.ds(pl.multiple_of(first, LANES), count)]
+    def arrived(slot, z_of, y_of, x_of, first, count, side=core):
+        piece = full.at[(z_of * 2 + y_of) * 4 + x_of * 2 + side, :, pl.ds(first, count)]
         pltpu.make_async_remote_copy(
             src_ref=piece, dst_ref=piece, send_sem=gather_send.at[slot], recv_sem=gather_recv.at[slot],
             device_id=sibling, device_id_type=MESH,
@@ -158,12 +141,19 @@
 
     def spread(step):
         z_of = flip_z(z, step)
-        send(X1 + step, z_of, y, x, my_col, half, x_side)
-        send(Y1 + step, z_of, y, x, my_col, half, y_side)
+        send(X1 + step, z_of, y, x, 0, half, x_side)
+        send(Y1 + step, z_of, y, x, 0, half, y_side)
 
     for step in (1, 2, 3):
-        send(Z + step, z, y, x, my_col, half, (flip_z(z, step) * 2 + y, inner))
+        send(Z + step, z, y, x, 0, half, (flip_z(z, step) * 2 + y, inner))
     spread(0)
+    send(CZ, z, y, x, 0, half, sibling)
+    swap.start()
+
+    def merge(low, high):
+        for block in range(pairs):
+            pair_rows[block, pl.ds(0, 8), :] = low[pl.ds(8 * block + 8, 8), :]
+            pair_rows[block, pl.ds(8, 8), :] = high[pl.ds(8 * block + 8, 8), :]
 
     chip_rows = pl.ds(pl.multiple_of(chip * 16, 16), 16)
 
@@ -171,7 +161,7 @@
         tile = 2 * index + core
         to_grp, to_inner = tile_owner(tile)
         copy = pltpu.make_async_remote_copy(
-            src_ref=pair_rows.at[pl.ds(1, pairs), :, pl.ds(pl.multiple_of(tile * LANES, LANES), LANES)],
+            src_ref=pair_rows.at[:, :, pl.ds(pl.multiple_of(tile * LANES, LANES), LANES)],
             dst_ref=left_cols.at[:, chip_rows, :],
             send_sem=left_send.at[index],
             recv_sem=left_recv.at[chip],
@@ -180,49 +170,60 @@
         )
         return to_grp * 2 + to_inner // 2 != chip, copy
 
-    @pl.loop(0, tiles // 2)
-    def _(step):
-        index = (step + 3 * (grp // 2)) % (tiles // 2)
-        away, copy = left_copy(index)
-
-        @pl.when(away)
+    def send_left():
+        swap.wait_recv()
+
+        @pl.when(core == 0)
         def _():
-            copy.start()
+            merge(own, sib)
+
+        @pl.when(core == 1)
+        def _():
+            merge(sib, own)
+
+        @pl.loop(0, tiles // 2)
+        def _(step):
+            index = (step + 3 * (grp // 2)) % (tiles // 2)
+            away, copy = left_copy(index)
+
+            @pl.when(away)
+            def _():
+                copy.start()
 
     def relay(step):
         z_of = flip_z(z, step)
-        arrived(X1 + step, z_of, y, 1 - x, my_col, half)
-        send(Y2 + step, z_of, y, 1 - x, my_col, quarter, y_side)
-        send(CX + step, z_of, y, 1 - x, my_col, half, sibling)
-        arrived(Y1 + step, z_of, 1 - y, x, my_col, half)
-        send(X2 + step, z_of, 1 - y, x, my_col + quarter, quarter, x_side)
-        send(CY + step, z_of, 1 - y, x, my_col, half, sibling)
+        arrived(X1 + step, z_of, y, 1 - x, 0, half)
+        send(Y2 + step, z_of, y, 1 - x, 0, quarter, y_side)
+        send(CX + step, z_of, y, 1 - x, 0, half, sibling)
+        arrived(Y1 + step, z_of, 1 - y, x, 0, half)
+        send(X2 + step, z_of, 1 - y, x, quarter, quarter, x_side)
+        send(CY + step, z_of, 1 - y, x, 0, half, sibling)
 
     def finish(step):
         z_of = flip_z(z, step)
-        arrived(Y2 + step, z_of, 1 - y, 1 - x, my_col, quarter)
-        arrived(X2 + step, z_of, 1 - y, 1 - x, my_col + quarter, quarter)
-        send(CD + step, z_of, 1 - y, 1 - x, my_col, half, sibling)
+        arrived(Y2 + step, z_of, 1 - y, 1 - x, 0, quarter)
+        arrived(X2 + step, z_of, 1 - y, 1 - x, quarter, quarter)
+        send(CD + step, z_of, 1 - y, 1 - x, 0, half, sibling)
 
     for step in (1, 2, 3):
         z_of = flip_z(z, step)
-        arrived(Z + step, z_of, y, x, my_col, half)
+        arrived(Z + step, z_of, y, x, 0, half)
         spread(step)
-        send(CZ + step, z_of, y, x, my_col, half, sibling)
+        send(CZ + step, z_of, y, x, 0, half, sibling)
         relay(step - 1)
+        if step == 2:
+            send_left()
         if step > 1:
             finish(step - 2)
     relay(3)
     finish(2)
     finish(3)
-    other_col = (1 - core) * half
     for step in range(4):
         z_of = flip_z(z, step)
-        if step:
-            arrived(CZ + step, z_of, y, x, other_col, half)
-        arrived(CX + step, z_of, y, 1 - x, other_col, half)
-        arrived(CY + step, z_of, 1 - y, x, other_col, half)
-        arrived(CD + step, z_of, 1 - y, 1 - x, other_col, half)
+        arrived(CZ + step, z_of, y, x, 0, half, 1 - core)
+        arrived(CX + step, z_of, y, 1 - x, 0, half, 1 - core)
+        arrived(CY + step, z_of, 1 - y, x, 0, half, 1 - core)
+        arrived(CD + step, z_of, 1 - y, 1 - x, 0, half, 1 - core)
 
     idle = 2 * ((z + y) % 2) + 1
     my_tile = grp * 3 + inner - jnp.where(inner > idle, 1, 0)
@@ -241,13 +242,13 @@
 
     @pl.when(inner != idle)
     def _():
-        left_cols[:, chip_rows, :] = pair_rows[pl.ds(1, pairs), :, my_lanes]
+        left_cols[:, chip_rows, :] = pair_rows[:, :, my_lanes]
 
         @pl.loop(1, 16)
         def _(step):
             source = (chip + step) % 16
             pltpu.make_async_remote_copy(
-                src_ref=pair_rows.at[pl.ds(1, pairs), :, pl.ds(0, LANES)],
+                src_ref=pair_rows.at[:, :, pl.ds(0, LANES)],
                 dst_ref=left_cols.at[:, pl.ds(pl.multiple_of(source * 16, 16), 16), :],
                 send_sem=left_send.at[0],
                 recv_sem=left_recv.at[source],
@@ -262,10 +263,12 @@
             shifts.append((occ_ref[left_ref[pair]] + occ_ref[second]) - vir_cols)
         shift = jnp.concatenate(shifts, axis=0)
         wide = 4 * LANES
-        total = jnp.zeros((pairs * LANES, full.shape[0]), jnp.float32)
+        total = jnp.zeros((pairs * LANES, left_rows.shape[1]), jnp.float32)
         for part in range(virtuals // wide):
             columns = pl.ds(part * wide, wide)
-            block = full[:, columns]
+            side, first = divmod(part * wide, half)
+            both = full[:, :, pl.ds(first, wide)].astype(jnp.float32)
+            block = both[:, 8 * side : 8 * side + 8].reshape(left_rows.shape[1], wide).astype(jnp.bfloat16)
             integral = jnp.dot(left_rows[...], block, preferred_element_type=jnp.float32)
             denominator = shift - vir_ref[:, columns]
             inverse = pl.reciprocal(denominator, approx=True)
@@ -310,12 +313,6 @@
                 device_id_type=MESH,
             ).wait_recv()
 
-    for orbital in range(gamma_ref.shape[0]):
-        row = jnp.where(left_ref[0] == orbital, out_ref[0], 0.0)
-        for pair in range(1, pairs):
-            row += jnp.where(left_ref[pair] == orbital, out_ref[pair], 0.0)
-        gamma_ref[orbital] = row
-
     @pl.when(inner != idle)
     def _():
         @pl.loop(1, 32)
@@ -329,9 +326,9 @@
     aux = 32 * aux_rows
     hbm, vmem = pl.BlockSpec(memory_space=pltpu.HBM), pl.BlockSpec(memory_space=pltpu.VMEM)
     dma = pltpu.SemaphoreType.DMA
-    return pl.pallas_call(
+    returned = pl.pallas_call(
         kernel,
-        out_shape=jax.ShapeDtypeStruct(b_tensor.shape, jnp.float32),
+        out_shape=jax.ShapeDtypeStruct((pairs, aux_rows, virtuals), jnp.float32),
         in_specs=[hbm] * 5,
         out_specs=vmem,
         scratch_shapes=[
@@ -341,11 +338,11 @@
             pltpu.SMEM(left_list.shape, jnp.int32),
             pltpu.SMEM(right_occ.shape, jnp.int32),
             dma((5,)),
-            pltpu.VMEM((pairs, aux_rows, virtuals), jnp.float32),
             pltpu.VMEM(((pairs + 1) * aux_rows, virtuals), jnp.bfloat16),
             pltpu.VMEM(((pairs + 1) * aux_rows, virtuals), jnp.bfloat16),
-            pltpu.VMEM((pairs + 1, 2 * aux_rows, virtuals), jnp.bfloat16),
-            pltpu.VMEM((aux, virtuals), jnp.bfloat16),
+            pltpu.VMEM((2 * aux_rows, virtuals // 2), jnp.bfloat16),
+            pltpu.VMEM((pairs, 2 * aux_rows, virtuals), jnp.bfloat16),
+            pltpu.VMEM((32, 2 * aux_rows, virtuals // 2), jnp.bfloat16),
             pltpu.VMEM((pairs, aux, LANES), jnp.bfloat16),
             pltpu.VMEM((pairs * LANES, aux), jnp.bfloat16),
             pltpu.VMEM((pairs, aux, LANES), jnp.float32),
@@ -359,6 +356,9 @@
             flops=4 * pairs * aux * virtuals * LANES, bytes_accessed=2 * occ_count * aux_rows * virtuals, transcendentals=0
         ),
     )(b_tensor, occ_energy, vir_energy.reshape(1, virtuals), left_list, right_occ)
+    orbitals = lax.broadcasted_iota(jnp.int32, (occ_count,) + returned.shape, 0)
+    chosen = orbitals == left_list[None, :, None, None]
+    return jnp.sum(jnp.where(chosen, returned[None], 0.0), axis=1)
 
 
 def solution(mesh):

time: 38.7 us -> 36.3 us (0.938)
  Pallas kernels: 35.7 us -> 33.1 us
  other arithmetic: 0 us -> 2.36 us
  local copies, waits for them, and re-layouts: 2.22 us -> 0.01 us
    pallas_call x1, Pallas kernels: 35.7 us -> 33.1 us  [body_tiles(): pl.pallas_call(kernel, out_shape=jax.ShapeDtypeStruct((pairs, aux_rows, v...]
    reduce_sum x0 -> x1, other arithmetic: none -> 2.36 us  [body_tiles(): return jnp.sum(jnp.where(chosen, returned[None], 0.0), axis=1)]
    unnamed x1 -> x2, local copies, waits for them, and re-layouts: 2.22 us -> 0.01 us
where the time goes in v4:
time: 36.3 us; the launch traced here: 36.1 us
  Pallas kernels  33.1 us (91%)
  other arithmetic  2.36 us (7%)
  between operations  0.68 us (2%)
    pallas_call x1, Pallas kernels, body_tiles(): pl.pallas_call(kernel, out_shape=jax.ShapeDtypeStruct((pairs, aux_rows, v...  33.1 us
    reduce_sum x1, other arithmetic, body_tiles(): return jnp.sum(jnp.where(chosen, returned[None], 0.0), axis=1)  2.36 us

profile of v4, /device:TPU:29, one launch (start us, length us, event | category | flops | bytes accessed | tf_op | source)
XLA Modules:
  0.0 36.1 jit_solution(13207249599838239476)
XLA Ops:
  0.7 0.0 copy-start
  0.7 33.1 %shard_map.55 = f32[3,8,3072]{2,1,0:T(8,128)} custom-call(bf16[10,8,3072]{2,1,0:T(8,128)(2,1)} %b_hbm.1, f32[10]{0:T(128)} %occ_hbm.1, f32[1,3072]{1,0:T(1,128)} %bitcast.1, s32[3]{0:T(128)} %left_hbm.1, s32[1]{0:T(128)S(6)} %copy.6.right_hbm), custom_call_target="tpu_custom_call" | custom-call | flops 1207959552 | bytes 491520 | tf_op jit(solution)/shard_map/pallas_call | solution.py:329
  33.8 0.0 copy-done
  33.8 2.4 %select_reduce_fusion = f32[10,8,3072]{2,1,0:T(8,128)} fusion(f32[3,8,3072]{2,1,0:T(8,128)} %shard_map.55, s32[3]{0:T(128)S(1)} %copy-done), kind=kLoop, calls=%fused_computation | loop fusion | flops 1966080 | bytes 1277964 | tf_op jit(solution)/shard_map/reduce_sum | solution.py:361
Async XLA Ops:
  0.7 33.1 %copy-start = (s32[3]{0:T(128)S(1)}, s32[3]{0:T(128)}, u32[]{:S(2)}) copy-start(s32[3]{0:T(128)} %left_hbm.1) | copy-start | bytes 40

commit v5 on v4

--- a/solution.py
+++ b/solution.py
@@ -183,7 +183,7 @@
 
         @pl.loop(0, tiles // 2)
         def _(step):
-            index = (step + 3 * (grp // 2)) % (tiles // 2)
+            index = (5 * step + 3 * z) % (tiles // 2)
             away, copy = left_copy(index)
 
             @pl.when(away)
@@ -230,7 +230,7 @@
     my_lanes = pl.ds(pl.multiple_of(my_tile * LANES, LANES), LANES)
 
     def out_copy(step):
-        other = (me + step) % 32
+        other = (me + 11 * step) % 32
         return pltpu.make_async_remote_copy(
             src_ref=contrib.at[:, pl.ds(pl.multiple_of(other * 8, 8), 8), :],
             dst_ref=out_ref.at[:, :, my_lanes],
@@ -318,6 +318,19 @@
         @pl.loop(1, 32)
         def _(step):
             out_copy(step).wait_send()
+
+
+def add_pairs(left_ref, returned_ref, gamma_ref, rows, sems):
+    copies = []
+    for orbital in range(rows.shape[0]):
+        row = jnp.where(left_ref[0] == orbital, returned_ref[0], 0.0)
+        for pair in range(1, returned_ref.shape[0]):
+            row += jnp.where(left_ref[pair] == orbital, returned_ref[pair], 0.0)
+        rows[orbital] = row
+        copies.append(pltpu.make_async_copy(rows.at[orbital], gamma_ref.at[orbital], sems.at[orbital]))
+        copies[-1].start()
+    for copy in copies:
+        copy.wait()
 
 
 def body_tiles(b_tensor, occ_energy, vir_energy, left_list, right_occ):
@@ -356,9 +369,13 @@
             flops=4 * pairs * aux * virtuals * LANES, bytes_accessed=2 * occ_count * aux_rows * virtuals, transcendentals=0
         ),
     )(b_tensor, occ_energy, vir_energy.reshape(1, virtuals), left_list, right_occ)
-    orbitals = lax.broadcasted_iota(jnp.int32, (occ_count,) + returned.shape, 0)
-    chosen = orbitals == left_list[None, :, None, None]
-    return jnp.sum(jnp.where(chosen, returned[None], 0.0), axis=1)
+    return pl.pallas_call(
+        add_pairs,
+        out_shape=jax.ShapeDtypeStruct(b_tensor.shape, jnp.float32),
+        in_specs=[pl.BlockSpec(memory_space=pltpu.SMEM), vmem],
+        out_specs=hbm,
+        scratch_shapes=[pltpu.VMEM(b_tensor.shape, jnp.float32), dma((occ_count,))],
+    )(left_list, returned)
 
 
 def solution(mesh):

time: 36.3 us -> 38.3 us (1.055)
  the two profiles are of different devices: /device:TPU:29 before, /device:TPU:0 now
where the time goes in v5:
time: 38.3 us; the launch traced here: 38.1 us
  Pallas kernels  37.4 us (98%)
  between operations  0.66 us (2%)
    pallas_call x1, Pallas kernels, body_tiles(): pl.pallas_call(kernel, out_shape=jax.ShapeDtypeStruct((pairs, aux_rows, v...  35.4 us
    pallas_call x1, Pallas kernels, body_tiles(): pl.pallas_call(add_pairs, out_shape=jax.ShapeDtypeStruct(b_tensor.shape,...  2.02 us

profile of v5, /device:TPU:0, one launch (start us, length us, event | category | flops | bytes accessed | tf_op | source)
XLA Modules:
  0.0 38.1 jit_solution(4506436165313594777)
XLA Ops:
  0.7 35.4 %shard_map.55.returned_ref = f32[3,8,3072]{2,1,0:T(8,128)} custom-call(bf16[10,8,3072]{2,1,0:T(8,128)(2,1)} %b_hbm.1, f32[10]{0:T(128)} %occ_hbm.1, f32[1,3072]{1,0:T(1,128)} %bitcast.1, s32[3]{0:T(128)} %left_ref.1, s32[1]{0:T(128)S(6)} %copy.6.right_hbm), custom_call_target="tpu_custom_call" | custom-call | flops 1207959552 | bytes 491520 | tf_op jit(solution)/shard_map/pallas_call | solution.py:342
  36.1 2.0 %shard_map.56 = f32[10,8,3072]{2,1,0:T(8,128)} custom-call(s32[3]{0:T(128)} %left_ref.1, f32[3,8,3072]{2,1,0:T(8,128)} %shard_map.55.returned_ref), custom_call_target="tpu_custom_call" | custom-call | tf_op jit(solution)/shard_map/pallas_call | solution.py:372

commit v6 on v5

--- a/solution.py
+++ b/solution.py
@@ -61,18 +61,16 @@
 
 
 def place(grp, inner):
-    return grp // 2, grp % 2, inner // 2, inner % 2
-
-
-def tile_owner(tile):
-    grp = tile // 3
-    slot = tile % 3
-    idle = 2 * ((grp // 2 + grp % 2) % 2) + 1
-    return grp, slot + jnp.where(slot >= idle, 1, 0)
+    z, x = lax.div(grp, 2), lax.div(inner, 2)
+    return z, grp - 2 * z, x, inner - 2 * x
+
+
+def idle_inner(z, y):
+    return 2 * lax.rem(z + y, 2) + 1
 
 
 def flip_z(z, step):
-    return (z, z + 1 - 2 * (z % 2), (z + 2) % 4, 3 - z)[step]
+    return (z, z + 1 - 2 * lax.rem(z, 2), lax.rem(z + 2, 4), 3 - z)[step]
 
 
 def kernel(
@@ -96,10 +94,13 @@
         fetch.start()
     barrier = pltpu.get_barrier_semaphore()
 
-    @pl.loop(1, 32)
-    def _(step):
-        other = (me + step) % 32
-        pl.semaphore_signal(barrier, inc=1, device_id=(other // 4, other % 4), device_id_type=MESH)
+    @pl.loop(0, 8)
+    def _(to_grp):
+        for to_inner in range(4):
+
+            @pl.when(to_grp * 4 + to_inner != me)
+            def _():
+                pl.semaphore_signal(barrier, inc=1, device_id=(to_grp, to_inner), device_id_type=MESH)
 
     for fetch in fetches:
         fetch.wait()
@@ -157,18 +158,33 @@
 
     chip_rows = pl.ds(pl.multiple_of(chip * 16, 16), 16)
 
-    def left_copy(index):
-        tile = 2 * index + core
-        to_grp, to_inner = tile_owner(tile)
-        copy = pltpu.make_async_remote_copy(
-            src_ref=pair_rows.at[:, :, pl.ds(pl.multiple_of(tile * LANES, LANES), LANES)],
-            dst_ref=left_cols.at[:, chip_rows, :],
-            send_sem=left_send.at[index],
-            recv_sem=left_recv.at[chip],
-            device_id=(to_grp, to_inner),
-            device_id_type=MESH,
-        )
-        return to_grp * 2 + to_inner // 2 != chip, copy
+    def for_left(act):
+        for side in range(2):
+
+            @pl.when(core == side)
+            def _():
+                @pl.loop(0, 4)
+                def _(step):
+                    to_z = lax.rem(z + step, 4)
+                    for to_y in range(2):
+                        for slot in range(3):
+                            if (to_y + slot) % 2 != side:
+                                continue
+                            to_grp = 2 * to_z + to_y
+                            tile = 3 * to_grp + slot
+                            to_inner = slot + jnp.where(slot >= idle_inner(to_z, to_y), 1, 0)
+                            copy = pltpu.make_async_remote_copy(
+                                src_ref=pair_rows.at[:, :, pl.ds(pl.multiple_of(tile * LANES, LANES), LANES)],
+                                dst_ref=left_cols.at[:, chip_rows, :],
+                                send_sem=left_send.at[tile],
+                                recv_sem=left_recv.at[chip],
+                                device_id=(to_grp, to_inner),
+                                device_id_type=MESH,
+                            )
+
+                            @pl.when(to_grp * 2 + lax.div(to_inner, 2) != chip)
+                            def _():
+                                act(copy)
 
     def send_left():
         swap.wait_recv()
@@ -181,14 +197,7 @@
         def _():
             merge(sib, own)
 
-        @pl.loop(0, tiles // 2)
-        def _(step):
-            index = (5 * step + 3 * z) % (tiles // 2)
-            away, copy = left_copy(index)
-
-            @pl.when(away)
-            def _():
-                copy.start()
+        for_left(lambda copy: copy.start())
 
     def relay(step):
         z_of = flip_z(z, step)
@@ -210,9 +219,9 @@
         arrived(Z + step, z_of, y, x, 0, half)
         spread(step)
         send(CZ + step, z_of, y, x, 0, half, sibling)
+        if step == 3:
+            send_left()
         relay(step - 1)
-        if step == 2:
-            send_left()
         if step > 1:
             finish(step - 2)
     relay(3)
@@ -225,20 +234,28 @@
         arrived(CY + step, z_of, 1 - y, x, 0, half, 1 - core)
         arrived(CD + step, z_of, 1 - y, 1 - x, 0, half, 1 - core)
 
-    idle = 2 * ((z + y) % 2) + 1
+    idle = idle_inner(z, y)
     my_tile = grp * 3 + inner - jnp.where(inner > idle, 1, 0)
     my_lanes = pl.ds(pl.multiple_of(my_tile * LANES, LANES), LANES)
 
-    def out_copy(step):
-        other = (me + 11 * step) % 32
-        return pltpu.make_async_remote_copy(
-            src_ref=contrib.at[:, pl.ds(pl.multiple_of(other * 8, 8), 8), :],
-            dst_ref=out_ref.at[:, :, my_lanes],
-            send_sem=out_send.at[step],
-            recv_sem=out_recv.at[my_tile],
-            device_id=(other // 4, other % 4),
-            device_id_type=MESH,
-        )
+    def for_out(act):
+        @pl.loop(0, 8)
+        def _(step):
+            to_grp = lax.rem(grp + step, 8)
+            for to_inner in range(4):
+                other = to_grp * 4 + to_inner
+                copy = pltpu.make_async_remote_copy(
+                    src_ref=contrib.at[:, pl.ds(pl.multiple_of(other * 8, 8), 8), :],
+                    dst_ref=out_ref.at[:, :, my_lanes],
+                    send_sem=out_send.at[other],
+                    recv_sem=out_recv.at[my_tile],
+                    device_id=(to_grp, to_inner),
+                    device_id_type=MESH,
+                )
+
+                @pl.when(other != me)
+                def _():
+                    act(copy)
 
     @pl.when(inner != idle)
     def _():
@@ -246,7 +263,7 @@
 
         @pl.loop(1, 16)
         def _(step):
-            source = (chip + step) % 16
+            source = lax.rem(chip + step, 16)
             pltpu.make_async_remote_copy(
                 src_ref=pair_rows.at[:, :, pl.ds(0, LANES)],
                 dst_ref=left_cols.at[:, pl.ds(pl.multiple_of(source * 16, 16), 16), :],
@@ -282,27 +299,18 @@
 
         out_ref[:, :, my_lanes] = contrib[:, pl.ds(pl.multiple_of(me * 8, 8), 8), :]
 
-        @pl.loop(1, 32)
-        def _(step):
-            out_copy(step).start()
+        for_out(lambda copy: copy.start())
 
     swap.wait_send()
     for copy in started:
         copy.wait_send()
 
-    @pl.loop(0, tiles // 2)
-    def _(index):
-        away, copy = left_copy(index)
-
-        @pl.when(away)
-        def _():
-            copy.wait_send()
+    for_left(lambda copy: copy.wait_send())
+    mine = jnp.where(inner == idle, -1, my_tile)
 
     @pl.loop(0, tiles)
     def _(tile):
-        from_grp, from_inner = tile_owner(tile)
-
-        @pl.when(from_grp * 4 + from_inner != me)
+        @pl.when(tile != mine)
         def _():
             pltpu.make_async_remote_copy(
                 src_ref=contrib.at[:, pl.ds(0, 8), :],
@@ -315,9 +323,7 @@
 
     @pl.when(inner != idle)
     def _():
-        @pl.loop(1, 32)
-        def _(step):
-            out_copy(step).wait_send()
+        for_out(lambda copy: copy.wait_send())
 
 
 def add_pairs(left_ref, returned_ref, gamma_ref, rows, sems):

time: 38.3 us -> 35.6 us (0.930)
  the two profiles are of different devices: /device:TPU:0 before, /device:TPU:29 now
where the time goes in v6:
time: 35.6 us; the launch traced here: 35.4 us
  Pallas kernels  34.8 us (98%)
  between operations  0.66 us (2%)
    pallas_call x1, Pallas kernels, body_tiles(): pl.pallas_call(kernel, out_shape=jax.ShapeDtypeStruct((pairs, aux_rows, v...  32.7 us
    pallas_call x1, Pallas kernels, body_tiles(): pl.pallas_call(add_pairs, out_shape=jax.ShapeDtypeStruct(b_tensor.shape,...  2.02 us

profile of v6, /device:TPU:29, one launch (start us, length us, event | category | flops | bytes accessed | tf_op | source)
XLA Modules:
  0.0 35.4 jit_solution(13628051645580467443)
XLA Ops:
  0.7 32.7 %shard_map.55.returned_ref = f32[3,8,3072]{2,1,0:T(8,128)} custom-call(bf16[10,8,3072]{2,1,0:T(8,128)(2,1)} %b_hbm.1, f32[10]{0:T(128)} %occ_hbm.1, f32[1,3072]{1,0:T(1,128)} %bitcast.1, s32[3]{0:T(128)} %left_ref.1, s32[1]{0:T(128)S(6)} %copy.6.right_hbm), custom_call_target="tpu_custom_call" | custom-call | flops 1207959552 | bytes 491520 | tf_op jit(solution)/shard_map/pallas_call | solution.py:348
  33.4 2.0 %shard_map.56 = f32[10,8,3072]{2,1,0:T(8,128)} custom-call(s32[3]{0:T(128)} %left_ref.1, f32[3,8,3072]{2,1,0:T(8,128)} %shard_map.55.returned_ref), custom_call_target="tpu_custom_call" | custom-call | tf_op jit(solution)/shard_map/pallas_call | solution.py:378

commit v7 on v6

--- a/solution.py
+++ b/solution.py
@@ -75,7 +75,7 @@
 
 def kernel(
     b_hbm, occ_hbm, vir_hbm, left_hbm, right_hbm, out_ref,
-    b_ref, occ_ref, vir_ref, left_ref, right_ref, input_sem, own, sib, folded, pair_rows, full, left_cols, left_rows, contrib,
+    b_ref, occ_ref, vir_ref, left_ref, right_ref, input_sem, own, sib, folded, pair_rows, full, left_cols, left_rows, plain, contrib,
     swap_send, swap_recv, gather_send, gather_recv, left_send, left_recv, out_send, out_recv,
 ):
     grp, inner = lax.axis_index("grp"), lax.axis_index("inner")
@@ -238,15 +238,15 @@
     my_tile = grp * 3 + inner - jnp.where(inner > idle, 1, 0)
     my_lanes = pl.ds(pl.multiple_of(my_tile * LANES, LANES), LANES)
 
-    def for_out(act):
+    def for_out(act, low=0, high=pairs):
         @pl.loop(0, 8)
         def _(step):
             to_grp = lax.rem(grp + step, 8)
             for to_inner in range(4):
                 other = to_grp * 4 + to_inner
                 copy = pltpu.make_async_remote_copy(
-                    src_ref=contrib.at[:, pl.ds(pl.multiple_of(other * 8, 8), 8), :],
-                    dst_ref=out_ref.at[:, :, my_lanes],
+                    src_ref=contrib.at[pl.ds(low, high - low), pl.ds(pl.multiple_of(other * 8, 8), 8), :],
+                    dst_ref=out_ref.at[pl.ds(low, high - low), :, my_lanes],
                     send_sem=out_send.at[other],
                     recv_sem=out_recv.at[my_tile],
                     device_id=(to_grp, to_inner),
@@ -278,28 +278,35 @@
         for pair in range(pairs):
             left_rows[pl.ds(pair * LANES, LANES), :] = jnp.transpose(left_cols[pair])
             shifts.append((occ_ref[left_ref[pair]] + occ_ref[second]) - vir_cols)
-        shift = jnp.concatenate(shifts, axis=0)
         wide = 4 * LANES
-        total = jnp.zeros((pairs * LANES, left_rows.shape[1]), jnp.float32)
-        for part in range(virtuals // wide):
-            columns = pl.ds(part * wide, wide)
-            side, first = divmod(part * wide, half)
-            both = full[:, :, pl.ds(first, wide)].astype(jnp.float32)
-            block = both[:, 8 * side : 8 * side + 8].reshape(left_rows.shape[1], wide).astype(jnp.bfloat16)
-            integral = jnp.dot(left_rows[...], block, preferred_element_type=jnp.float32)
-            denominator = shift - vir_ref[:, columns]
-            inverse = pl.reciprocal(denominator, approx=True)
-            inverse = inverse * (2.0 - denominator * inverse)
-            amplitude = (integral * inverse).astype(jnp.bfloat16)
-            total += lax.dot_general(
-                amplitude, block, (((1,), (1,)), ((), ())), preferred_element_type=jnp.float32
-            )
-        for pair in range(pairs):
-            contrib[pair] = jnp.transpose(total[pair * LANES : (pair + 1) * LANES])
-
-        out_ref[:, :, my_lanes] = contrib[:, pl.ds(pl.multiple_of(me * 8, 8), 8), :]
-
-        for_out(lambda copy: copy.start())
+
+        def work(low, high):
+            shift = jnp.concatenate(shifts[low:high], axis=0)
+            left = left_rows[pl.ds(low * LANES, (high - low) * LANES), :]
+            total = jnp.zeros(left.shape, jnp.float32)
+            for part in range(virtuals // wide):
+                columns = pl.ds(part * wide, wide)
+                if low == 0:
+                    side, first = divmod(part * wide, half)
+                    block = full[:, pl.ds(8 * side, 8), pl.ds(first, wide)].astype(jnp.float32)
+                    plain[:, columns] = block.reshape(plain.shape[0], wide).astype(jnp.bfloat16)
+                block = plain[:, columns]
+                integral = jnp.dot(left, block, preferred_element_type=jnp.float32)
+                denominator = shift - vir_ref[:, columns]
+                inverse = pl.reciprocal(denominator, approx=True)
+                inverse = inverse * (2.0 - denominator * inverse)
+                amplitude = (integral * inverse).astype(jnp.bfloat16)
+                total += lax.dot_general(
+                    amplitude, block, (((1,), (1,)), ((), ())), preferred_element_type=jnp.float32
+                )
+            for pair in range(low, high):
+                first = (pair - low) * LANES
+                contrib[pair] = jnp.transpose(total[first : first + LANES])
+                out_ref[pair, :, my_lanes] = contrib[pair, pl.ds(pl.multiple_of(me * 8, 8), 8), :]
+            for_out(lambda copy: copy.start(), low, high)
+
+        work(0, 1)
+        work(1, pairs)
 
     swap.wait_send()
     for copy in started:
@@ -364,6 +371,7 @@
             pltpu.VMEM((32, 2 * aux_rows, virtuals // 2), jnp.bfloat16),
             pltpu.VMEM((pairs, aux, LANES), jnp.bfloat16),
             pltpu.VMEM((pairs * LANES, aux), jnp.bfloat16),
+            pltpu.VMEM((aux, virtuals), jnp.bfloat16),
             pltpu.VMEM((pairs, aux, LANES), jnp.float32),
             dma, dma, dma((36,)), dma((36,)), dma((virtuals // LANES,)), dma((16,)),
             dma((32,)), dma((virtuals // LANES,)),

time: 35.6 us -> 35.3 us (level)
  the two profiles are of different devices: /device:TPU:29 before, /device:TPU:0 now
where the time goes in v7:
time: 35.3 us; the launch traced here: 34.8 us
  Pallas kernels  34.1 us (97%)
  between operations  0.66 us (2%)
    pallas_call x1, Pallas kernels, body_tiles(): pl.pallas_call(kernel, out_shape=jax.ShapeDtypeStruct((pairs, aux_rows, v...  32.1 us
    pallas_call x1, Pallas kernels, body_tiles(): pl.pallas_call(add_pairs, out_shape=jax.ShapeDtypeStruct(b_tensor.shape,...  2.02 us

profile of v7, /device:TPU:0, one launch (start us, length us, event | category | flops | bytes accessed | tf_op | source)
XLA Modules:
  0.0 34.8 jit_solution(17738060199455399578)
XLA Ops:
  0.7 32.1 %shard_map.55.returned_ref = f32[3,8,3072]{2,1,0:T(8,128)} custom-call(bf16[10,8,3072]{2,1,0:T(8,128)(2,1)} %b_hbm.1, f32[10]{0:T(128)} %occ_hbm.1, f32[1,3072]{1,0:T(1,128)} %bitcast.1, s32[3]{0:T(128)} %left_ref.1, s32[1]{0:T(128)S(6)} %copy.6.right_hbm), custom_call_target="tpu_custom_call" | custom-call | flops 1207959552 | bytes 491520 | tf_op jit(solution)/shard_map/pallas_call | solution.py:355
  32.8 2.0 %shard_map.56 = f32[10,8,3072]{2,1,0:T(8,128)} custom-call(s32[3]{0:T(128)} %left_ref.1, f32[3,8,3072]{2,1,0:T(8,128)} %shard_map.55.returned_ref), custom_call_target="tpu_custom_call" | custom-call | tf_op jit(solution)/shard_map/pallas_call | solution.py:386

commit v8 on v7

--- a/solution.py
+++ b/solution.py
@@ -85,7 +85,6 @@
     pairs = out_ref.shape[0]
     half = full.shape[2]
     virtuals = 2 * half
-    quarter = half // 2
     tiles = virtuals // LANES
 
     inputs = ((b_hbm, b_ref), (occ_hbm, occ_ref), (vir_hbm, vir_ref), (left_hbm, left_ref), (right_hbm, right_ref))
@@ -120,6 +119,7 @@
 
     x_side = (grp, (1 - x) * 2 + core)
     y_side = (z * 2 + 1 - y, inner)
+    xy_side = (z * 2 + 1 - y, (1 - x) * 2 + core)
     started = []
 
     def send(slot, z_of, y_of, x_of, first, count, target):
@@ -138,10 +138,11 @@
             device_id=sibling, device_id_type=MESH,
         ).wait_recv()
 
-    Z, X1, Y1, X2, Y2, CZ, CX, CY, CD = 0, 4, 8, 12, 16, 20, 24, 28, 32
+    Z, X1, Y1, D1, CZ, CX, CY, CD = 0, 4, 8, 12, 16, 20, 24, 28
 
     def spread(step):
         z_of = flip_z(z, step)
+        send(D1 + step, z_of, y, x, 0, half, xy_side)
         send(X1 + step, z_of, y, x, 0, half, x_side)
         send(Y1 + step, z_of, y, x, 0, half, y_side)
 
@@ -201,18 +202,9 @@
 
     def relay(step):
         z_of = flip_z(z, step)
-        arrived(X1 + step, z_of, y, 1 - x, 0, half)
-        send(Y2 + step, z_of, y, 1 - x, 0, quarter, y_side)
-        send(CX + step, z_of, y, 1 - x, 0, half, sibling)
-        arrived(Y1 + step, z_of, 1 - y, x, 0, half)
-        send(X2 + step, z_of, 1 - y, x, quarter, quarter, x_side)
-        send(CY + step, z_of, 1 - y, x, 0, half, sibling)
-
-    def finish(step):
-        z_of = flip_z(z, step)
-        arrived(Y2 + step, z_of, 1 - y, 1 - x, 0, quarter)
-        arrived(X2 + step, z_of, 1 - y, 1 - x, quarter, quarter)
-        send(CD + step, z_of, 1 - y, 1 - x, 0, half, sibling)
+        for slot, onward, y_of, x_of in ((X1, CX, y, 1 - x), (Y1, CY, 1 - y, x), (D1, CD, 1 - y, 1 - x)):
+            arrived(slot + step, z_of, y_of, x_of, 0, half)
+            send(onward + step, z_of, y_of, x_of, 0, half, sibling)
 
     for step in (1, 2, 3):
         z_of = flip_z(z, step)
@@ -222,11 +214,7 @@
         if step == 3:
             send_left()
         relay(step - 1)
-        if step > 1:
-            finish(step - 2)
     relay(3)
-    finish(2)
-    finish(3)
     for step in range(4):
         z_of = flip_z(z, step)
         arrived(CZ + step, z_of, y, x, 0, half, 1 - core)
@@ -373,7 +361,7 @@
             pltpu.VMEM((pairs * LANES, aux), jnp.bfloat16),
             pltpu.VMEM((aux, virtuals), jnp.bfloat16),
             pltpu.VMEM((pairs, aux, LANES), jnp.float32),
-            dma, dma, dma((36,)), dma((36,)), dma((virtuals // LANES,)), dma((16,)),
+            dma, dma, dma((32,)), dma((32,)), dma((virtuals // LANES,)), dma((16,)),
             dma((32,)), dma((virtuals // LANES,)),
         ],
         compiler_params=pltpu.CompilerParams(

time: 35.3 us -> 34.8 us (0.986)
  no operation moved by 1% of the time
where the time goes in v8:
time: 34.8 us; the launch traced here: 34.6 us
  Pallas kernels  34 us (98%)
  between operations  0.66 us (2%)
    pallas_call x1, Pallas kernels, body_tiles(): pl.pallas_call(kernel, out_shape=jax.ShapeDtypeStruct((pairs, aux_rows, v...  32 us
    pallas_call x1, Pallas kernels, body_tiles(): pl.pallas_call(add_pairs, out_shape=jax.ShapeDtypeStruct(b_tensor.shape,...  2.02 us

profile of v8, /device:TPU:0, one launch (start us, length us, event | category | flops | bytes accessed | tf_op | source)
XLA Modules:
  0.0 34.6 jit_solution(7447156180586370792)
XLA Ops:
  0.7 32.0 %shard_map.55.returned_ref = f32[3,8,3072]{2,1,0:T(8,128)} custom-call(bf16[10,8,3072]{2,1,0:T(8,128)(2,1)} %b_hbm.1, f32[10]{0:T(128)} %occ_hbm.1, f32[1,3072]{1,0:T(1,128)} %bitcast.1, s32[3]{0:T(128)} %left_ref.1, s32[1]{0:T(128)S(6)} %copy.6.right_hbm), custom_call_target="tpu_custom_call" | custom-call | flops 1207959552 | bytes 491520 | tf_op jit(solution)/shard_map/pallas_call | solution.py:343
  32.6 2.0 %shard_map.56 = f32[10,8,3072]{2,1,0:T(8,128)} custom-call(s32[3]{0:T(128)} %left_ref.1, f32[3,8,3072]{2,1,0:T(8,128)} %shard_map.55.returned_ref), custom_call_target="tpu_custom_call" | custom-call | tf_op jit(solution)/shard_map/pallas_call | solution.py:374

commit v9 on v8

--- a/solution.py
+++ b/solution.py
@@ -229,7 +229,7 @@
     def for_out(act, low=0, high=pairs):
         @pl.loop(0, 8)
         def _(step):
-            to_grp = lax.rem(grp + step, 8)
+            to_grp = lax.rem(grp + 4 + step, 8)
             for to_inner in range(4):
                 other = to_grp * 4 + to_inner
                 copy = pltpu.make_async_remote_copy(

time: 34.8 us -> 36 us (1.034)
  Pallas kernels: 34 us -> 35.2 us
    pallas_call x1, Pallas kernels: 32 us -> 33.2 us  [body_tiles(): pl.pallas_call(kernel, out_shape=jax.ShapeDtypeStruct((pairs, aux_rows, v...]
where the time goes in v9:
time: 36 us; the launch traced here: 35.9 us
  Pallas kernels  35.2 us (98%)
  between operations  0.66 us (2%)
    pallas_call x1, Pallas kernels, body_tiles(): pl.pallas_call(kernel, out_shape=jax.ShapeDtypeStruct((pairs, aux_rows, v...  33.2 us
    pallas_call x1, Pallas kernels, body_tiles(): pl.pallas_call(add_pairs, out_shape=jax.ShapeDtypeStruct(b_tensor.shape,...  2.02 us

profile of v9, /device:TPU:0, one launch (start us, length us, event | category | flops | bytes accessed | tf_op | source)
XLA Modules:
  0.0 35.9 jit_solution(8409858059318421941)
XLA Ops:
  0.7 33.2 %shard_map.55.returned_ref = f32[3,8,3072]{2,1,0:T(8,128)} custom-call(bf16[10,8,3072]{2,1,0:T(8,128)(2,1)} %b_hbm.1, f32[10]{0:T(128)} %occ_hbm.1, f32[1,3072]{1,0:T(1,128)} %bitcast.1, s32[3]{0:T(128)} %left_ref.1, s32[1]{0:T(128)S(6)} %copy.6.right_hbm), custom_call_target="tpu_custom_call" | custom-call | flops 1207959552 | bytes 491520 | tf_op jit(solution)/shard_map/pallas_call | solution.py:343
  33.9 2.0 %shard_map.56 = f32[10,8,3072]{2,1,0:T(8,128)} custom-call(s32[3]{0:T(128)} %left_ref.1, f32[3,8,3072]{2,1,0:T(8,128)} %shard_map.55.returned_ref), custom_call_target="tpu_custom_call" | custom-call | tf_op jit(solution)/shard_map/pallas_call | solution.py:374

commit v10 on v8

--- a/solution.py
+++ b/solution.py
@@ -142,9 +142,9 @@
 
     def spread(step):
         z_of = flip_z(z, step)
-        send(D1 + step, z_of, y, x, 0, half, xy_side)
         send(X1 + step, z_of, y, x, 0, half, x_side)
         send(Y1 + step, z_of, y, x, 0, half, y_side)
+        send(D1 + step, z_of, y, x, 0, half, xy_side)
 
     for step in (1, 2, 3):
         send(Z + step, z, y, x, 0, half, (flip_z(z, step) * 2 + y, inner))

time: 34.8 us -> 34.4 us (0.989)
  Pallas kernels: 34 us -> 33.6 us
    pallas_call x1, Pallas kernels: 32 us -> 31.6 us  [body_tiles(): pl.pallas_call(kernel, out_shape=jax.ShapeDtypeStruct((pairs, aux_rows, v...]
where the time goes in v10:
time: 34.4 us; the launch traced here: 34.2 us
  Pallas kernels  33.6 us (98%)
  between operations  0.66 us (2%)
    pallas_call x1, Pallas kernels, body_tiles(): pl.pallas_call(kernel, out_shape=jax.ShapeDtypeStruct((pairs, aux_rows, v...  31.6 us
    pallas_call x1, Pallas kernels, body_tiles(): pl.pallas_call(add_pairs, out_shape=jax.ShapeDtypeStruct(b_tensor.shape,...  2.02 us

profile of v10, /device:TPU:0, one launch (start us, length us, event | category | flops | bytes accessed | tf_op | source)
XLA Modules:
  0.0 34.2 jit_solution(7699531762560110997)
XLA Ops:
  0.7 31.6 %shard_map.55.returned_ref = f32[3,8,3072]{2,1,0:T(8,128)} custom-call(bf16[10,8,3072]{2,1,0:T(8,128)(2,1)} %b_hbm.1, f32[10]{0:T(128)} %occ_hbm.1, f32[1,3072]{1,0:T(1,128)} %bitcast.1, s32[3]{0:T(128)} %left_ref.1, s32[1]{0:T(128)S(6)} %copy.6.right_hbm), custom_call_target="tpu_custom_call" | custom-call | flops 1207959552 | bytes 491520 | tf_op jit(solution)/shard_map/pallas_call | solution.py:343
  32.2 2.0 %shard_map.56 = f32[10,8,3072]{2,1,0:T(8,128)} custom-call(s32[3]{0:T(128)} %left_ref.1, f32[3,8,3072]{2,1,0:T(8,128)} %shard_map.55.returned_ref), custom_call_target="tpu_custom_call" | custom-call | tf_op jit(solution)/shard_map/pallas_call | solution.py:374
